TPU v7x, 256 devices: a whole 4x4x8 slice. The times are simulated.
256 devices in a mesh: view: 8 (over x, core), band: 32 (over z, y).
Axes of the slice: x: 4, y: 4, z: 8, core: 2. Of those that a mesh axis runs over, the one named last changes fastest.
Arguments:
- latents: bfloat16 [8, 8192, 1024], P('view', 'band'), may hold values from -170 to 170
- w_qkv: bfloat16 [1024, 3072], replicated, may hold values from -0.75 to 0.75
- w_out: bfloat16 [1024, 1024], replicated, may hold values from -0.1875 to 0.1875
- epipolar_bands: int32 [8, 32, 8], replicated, may hold values from -1 to 31, as said below
- object_token_mask: int32 [8, 8192], replicated, may hold values from 0 to 1, as said below
Outputs:
- updated: float32 [8, 8192, 1024], P('view', 'band')
Inputs may be any that keep to these rules, and one draw needn't show every extreme that they name: epipolar_bands[v, b, w] is -1 where w is v or the epipolar lines miss view w; otherwise a band of view w within 2 bands of b. For every query band and every nonzero distance d, at most 2 views have band b + d listed, and some query band lists 2 views at one such distance. `object_token_mask`: the first token of every band is 1.
All inputs are finite; a program needn't handle non-finite values.
Results may differ from a plain program's by a relative error of at most 0.023.
Values may be sent and summed in bfloat16 or wider, within the bound.
A program may use at most 128 MiB of HBM per device.

v0:
```python
import jax
import jax.numpy as jnp
from jax import lax
from jax.sharding import PartitionSpec as P

HEADS = 16
HEAD_DIM = 64
REACH = 2
MOST = 2


def with_halo(cells, sides, width):
    for axis, dim in sides:
        count = lax.axis_size(axis)
        ends = count - 1
        head = lax.slice_in_dim(cells, 0, width, axis=dim)
        tail = lax.slice_in_dim(cells, cells.shape[dim] - width, cells.shape[dim], axis=dim)
        cells = jnp.concatenate(
            [
                lax.ppermute(tail, axis, [(i, (i + 1) % count) for i in range(ends)]),
                cells,
                lax.ppermute(head, axis, [((i + 1) % count, i) for i in range(ends)]),
            ],
            axis=dim,
        )
    return cells


def from_behind(block, axis, distance):
    devices = range(lax.axis_size(axis))
    route = [(i - distance, i) for i in devices if i - distance in devices]
    return lax.ppermute(block, axis, route)


def attend_heads(queries, key_rows, values, usable):
    count_of_rows = queries.shape[0]
    key_count = key_rows.shape[0]
    groups = HEADS // 4
    score_scale = HEAD_DIM ** (-0.5)
    query_parts = queries.reshape(count_of_rows, groups, 4, HEAD_DIM).transpose(1, 0, 2, 3)
    key_parts = key_rows.reshape(key_count, groups, 4, HEAD_DIM).transpose(1, 0, 2, 3)
    value_parts = values.reshape(key_count, groups, 4, HEAD_DIM).transpose(1, 0, 2, 3)

    def per_group(operands):
        query_block, key_block, value_block = operands
        scores = (
            jnp.einsum("qhd,khd->hqk", query_block, key_block, preferred_element_type=jnp.float32)
            * score_scale
        )
        scores = jnp.where(usable[None, None, :], scores, -1e30)
        row_top = jnp.max(scores, axis=-1, keepdims=True)
        raised = jnp.exp(scores - row_top)
        attention = (raised / jnp.sum(raised, axis=-1, keepdims=True)).astype(jnp.bfloat16)
        return jnp.einsum(
            "hqk,khd->qhd", attention, value_block, preferred_element_type=jnp.float32
        )

    blended = lax.map(per_group, (query_parts, key_parts, value_parts))
    return (
        blended.transpose(1, 0, 2, 3).reshape(count_of_rows, HEADS * HEAD_DIM).astype(jnp.bfloat16)
    )


def offset_payload(offset, pick_from, epipolar_bands, local_view, my_band, band_list):
    slot_ids = jnp.arange(MOST, dtype=jnp.int32)
    requester = my_band - offset
    inside = (requester >= 0) & (requester < band_list)
    wanted = epipolar_bands[local_view, jnp.clip(requester, 0, band_list - 1)]
    matches = (wanted == my_band) & inside
    match_count = matches.astype(jnp.int32)
    ranks = jnp.cumsum(match_count) - match_count
    picker = (matches[None, :] & (ranks[None, :] == slot_ids[:, None])).astype(jnp.bfloat16)
    return jnp.einsum("rw,wtc->rtc", picker, pick_from, preferred_element_type=jnp.float32).astype(
        jnp.bfloat16
    )


def locate_slabs(stacked, local_list, my_band, view_list):
    view_numbers = jnp.arange(view_list, dtype=jnp.int32)
    distance = local_list - my_band
    present = local_list >= 0
    same_shift = (
        (distance[:, None] == distance[None, :])
        & present[None, :]
        & (view_numbers[None, :] < view_numbers[:, None])
    )
    my_ranks = jnp.sum(same_shift.astype(jnp.int32), axis=1)
    position = jnp.where(distance < 0, distance + REACH, distance + REACH - 1)
    location = jnp.where(distance == 0, view_numbers, view_list + position * MOST + my_ranks)
    location = jnp.where(present, location, 0)
    return jnp.take(stacked, location, axis=0)


def body(latents, w_qkv, w_out, epipolar_bands, object_token_mask):
    view_list = lax.axis_size("view")
    band_list = lax.axis_size("band")
    local_view = lax.axis_index("view")
    my_band = lax.axis_index("band")
    count_of_rows = latents.shape[1]
    width = latents.shape[2]
    tokens = latents[0]
    projected = jnp.dot(tokens, w_qkv, preferred_element_type=jnp.float32).astype(jnp.bfloat16)
    queries = projected[:, :width]
    key_value = projected[:, width:]
    active_flags = object_token_mask.reshape(view_list, band_list, count_of_rows) > 0
    local_list = epipolar_bands[local_view, my_band]
    view_numbers = jnp.arange(view_list, dtype=jnp.int32)
    nonzero = [distance_step for distance_step in range(-REACH, REACH + 1) if distance_step != 0]
    nearby = with_halo(key_value[None], (("band", 0),), 1)
    gathered = lax.all_gather(key_value[None], "view", axis=0, tiled=True)
    sources = [gathered]
    for offset in nonzero:
        payload = offset_payload(offset, gathered, epipolar_bands, local_view, my_band, band_list)
        sources.append(from_behind(payload, "band", -offset))
    epipolar = locate_slabs(jnp.concatenate(sources, axis=0), local_list, my_band, view_list)
    slabs = jnp.concatenate([nearby, epipolar], axis=0)
    neighbour_index = my_band + jnp.arange(-1, 2, dtype=jnp.int32)
    neighbour_inside = (neighbour_index >= 0) & (neighbour_index < band_list)
    neighbour_active = (
        active_flags[local_view, jnp.clip(neighbour_index, 0, band_list - 1)]
        & neighbour_inside[:, None]
    )
    far_live = (
        active_flags[view_numbers, jnp.clip(local_list, 0, band_list - 1)]
        & (local_list >= 0)[:, None]
        & (view_numbers != local_view)[:, None]
    )
    usable = jnp.concatenate([neighbour_active, far_live], axis=0).reshape(-1)
    flattened = slabs.reshape(-1, 2 * width)
    blended = attend_heads(queries, flattened[:, :width], flattened[:, width:], usable)
    updated = tokens.astype(jnp.float32) + jnp.dot(
        blended, w_out, preferred_element_type=jnp.float32
    )
    return updated[None]


def solution(mesh):
    placed = (P("view", "band", None), P(), P(), P(), P())
    return jax.shard_map(
        body, mesh=mesh, in_specs=placed, out_specs=P("view", "band", None), check_vma=False
    )
```

profile of v0, /device:TPU:1, one launch (start us, length us, event | category | flops | bytes accessed | tf_op | source)
XLA Modules:
  0.0 399.5 jit_solution(18044199207738665563)
XLA Ops:
  6.5 4.9 %convolution_convert_fusion = bf16[256,3072]{1,0:T(8,128)(2,1)S(1)} fusion(bf16[1024,3072]{1,0:T(8,128)(2,1)} %param.8, bf16[1,256,1024]{2,1,0:T(8,128)(2,1)} %param.7), kind=kOutput, calls=%fused_computation.41 | convolution fusion | flops 1611399168 | bytes 8388608 | tf_op jit(solution)/shard_map/dot_general | solution.py:102
  11.5 1.1 copy-done.2
  12.6 1.2 slice_bitcast_fusion
  13.8 1.3 collective-permute-start.1
  15.2 1.9 slice.24
  17.1 0.3 clamp_reduce_fusion
  17.9 0.2 reduce-window.33
  18.1 0.2 reduce-window.32
  18.2 0.2 reduce-window.35
  18.4 0.2 reduce-window.34
  18.7 0.6 gather_fusion.1
  19.3 0.2 compare_reduce_fusion
  19.5 0.2 convert_reduce_fusion.4
  19.7 0.6 gather_fusion.2
  20.5 2.0 copy.37
  22.6 47.9 %all-gather.3.cloned.1.call-done = bf16[2048,2048]{1,0:T(8,128)(2,1)} async-done(((bf16[256,2048]{1,0:T(8,128)(2,1)}), bf16[2048,2048]{1,0:T(8,128)(2,1)}) %all-gather.3.cloned.1.call-update) | async-done | bytes 8388624 | tf_op jit(solution)/shard_map/all_gather | solution.py:110
  70.5 10.9 %fusion.50 = bf16[2,256,2048]{2,0,1:T(2,128)(2,1)} fusion(bf16[8,256,2048]{2,1,0:T(8,128)(2,1)} %bitcast.134, pred[8]{0:T(512)(128)(4,1)S(1)} %reduce.2, s32[8]{0:T(128)S(1)} %bitcast_subtract_fusion.3), kind=kOutput, calls=%fused_computation.42 | convolution fusion | flops 17825824 | bytes 10485800 | tf_op jit(solution)/shard_map/rw,wtc->rtc/dot_general | solution.py:73
  81.4 6.0 %collective-permute-start.2 = (bf16[2,256,2048]{2,0,1:T(2,128)(2,1)}, bf16[2,256,2048]{2,0,1:T(2,128)(2,1)}, u32[]{:S(2)}, u32[]{:S(2)}) collective-permute-start(bf16[2,256,2048]{2,0,1:T(2,128)(2,1)} %fusion.50), channel_id=1, source_target_pairs={{0,2},{1,3},{2,4},{3,5},{4,6},{5,7},{6,8},{7,9},{8,10},{9,11},{10,... | collective-permute-start | bytes 6291464 | tf_op jit(solution)/shard_map/ppermute | solution.py:32
  87.4 7.0 %fusion.53 = bf16[2,256,2048]{2,0,1:T(2,128)(2,1)} fusion(bf16[8,256,2048]{2,1,0:T(8,128)(2,1)S(1)} %bitcast.136, pred[8]{0:T(512)(128)(4,1)S(1)} %reduce.4, s32[8]{0:T(128)S(1)} %bitcast_subtract_fusion.2), kind=kOutput, calls=%fused_computation.43 | convolution fusion | flops 17825824 | bytes 10485800 | tf_op jit(solution)/shard_map/rw,wtc->rtc/dot_general | solution.py:73
  94.4 3.5 collective-permute-start.3
  97.9 7.0 %fusion.56 = bf16[2,256,2048]{2,0,1:T(2,128)(2,1)} fusion(bf16[8,256,2048]{2,1,0:T(8,128)(2,1)S(1)} %bitcast.137, pred[8]{0:T(512)(128)(4,1)S(1)} %reduce.6, s32[8]{0:T(128)S(1)} %bitcast_subtract_fusion.1), kind=kOutput, calls=%fused_computation.44 | convolution fusion | flops 17825824 | bytes 10485800 | tf_op jit(solution)/shard_map/rw,wtc->rtc/dot_general | solution.py:73
  104.9 1.3 collective-permute-start.4
  106.2 7.0 %fusion.59 = bf16[2,256,2048]{2,0,1:T(2,128)(2,1)} fusion(bf16[8,256,2048]{2,1,0:T(8,128)(2,1)S(1)} %bitcast.138, pred[8]{0:T(512)(128)(4,1)S(1)} %reduce.8, s32[8]{0:T(128)S(1)} %bitcast_subtract_fusion), kind=kOutput, calls=%fused_computation.45 | convolution fusion | flops 17825824 | bytes 10485800 | tf_op jit(solution)/shard_map/rw,wtc->rtc/dot_general | solution.py:73
  113.2 1.3 collective-permute-start.5
  114.5 8.3 %constant_dynamic-update-slice_fusion = bf16[16,256,2048]{2,1,0:T(8,128)(2,1)} fusion(bf16[8,256,2048]{2,1,0:T(8,128)(2,1)} %bitcast.135), kind=kLoop, calls=%fused_computation.56 | loop fusion | bytes 16777216
  122.8 8.4 %collective-permute-done.2 = bf16[2,256,2048]{2,0,1:T(2,128)(2,1)} collective-permute-done((bf16[2,256,2048]{2,0,1:T(2,128)(2,1)}, bf16[2,256,2048]{2,0,1:T(2,128)(2,1)}, u32[]{:S(2)}, u32[]{:S(2)}) %collective-permute-start.2) | collective-permute-done | bytes 2097184 | tf_op jit(solution)/shard_map/ppermute | solution.py:32
  131.2 93.0 %collective-permute-start = (bf16[1,256,2048]{2,1,0:T(8,128)(2,1)S(1)}, bf16[1,256,2048]{2,1,0:T(8,128)(2,1)}, u32[]{:S(2)}, u32[]{:S(2)}) collective-permute-start(bf16[1,256,2048]{2,1,0:T(8,128)(2,1)S(1)} %get-tuple-element.67), channel_id=1, source_target_pairs={{0,1},{1,2},{2,3},{3,4},{4,5},{5,6},{6,7},{7,8},{8,9},{9,10},{10,1... | collective-permute-start | bytes 3145736 | tf_op jit(solution)/shard_map/ppermute | solution.py:20
  224.1 3.9 copy_dynamic-update-slice_fusion.3
  228.0 3.8 copy_dynamic-update-slice_fusion.2
  231.8 35.2 %collective-permute-done.4 = bf16[2,256,2048]{2,0,1:T(2,128)(2,1)} collective-permute-done((bf16[2,256,2048]{2,0,1:T(2,128)(2,1)}, bf16[2,256,2048]{2,0,1:T(2,128)(2,1)}, u32[]{:S(2)}, u32[]{:S(2)}) %collective-permute-start.4) | collective-permute-done | bytes 2097184 | tf_op jit(solution)/shard_map/ppermute | solution.py:32
  266.9 3.8 copy_dynamic-update-slice_fusion.1
  270.8 2.2 copy_dynamic-update-slice_fusion
  273.0 10.4 %gather_fusion = bf16[8,256,2048]{2,1,0:T(8,128)(2,1)} fusion(bf16[16,256,2048]{2,1,0:T(8,128)(2,1)} %copy_dynamic-update-slice_fusion, s32[1024]{0:T(1024)S(1)} %pad_clamp_fusion), kind=kCustom, calls=%fused_computation | custom fusion | bytes 16777248 | tf_op jit(solution)/shard_map/jit(_take)/gather | solution.py:91
  283.4 7.5 %broadcast_select_fusion = bf16[8,256,2048]{2,1,0:T(8,128)(2,1)} fusion(bf16[8,256,2048]{2,1,0:T(8,128)(2,1)} %gather_fusion, pred[8]{0:T(512)(128)(4,1)S(1)} %compare_and_fusion.1), kind=kLoop, calls=%fused_computation.32 | loop fusion | flops 4194304 | bytes 16777224 | tf_op jit(solution)/shard_map/jit(_take)/select_n | solution.py:91
  290.9 9.5 %pad_maximum_fusion = bf16[11,256,2048]{2,1,0:T(8,128)(2,1)} fusion(bf16[8,256,2048]{2,1,0:T(8,128)(2,1)} %broadcast_select_fusion, bf16[1,256,2048]{2,1,0:T(8,128)(2,1)} %collective-permute-done.1, bf16[1,256,2048]{2,1,0:T(8,128)(2,1)S(1)} %get-tuple-element.67, bf16[1,256,2048]{2,1,0:T(8,128)(2,1)} %collective-permute-done), kind=kLoop, calls=%fused_computation.31 | loop fusion | flops 17301504 | bytes 23068672 | tf_op jit(solution)/shard_map/concatenate | solution.py:116
  300.4 10.0 %fusion.117 = (bf16[2816,1024]{1,0:T(8,128)(2,1)}, bf16[2816,1024]{1,0:T(8,128)(2,1)}) fusion(bf16[2816,2048]{1,0:T(8,128)(2,1)} %bitcast.139), kind=kLoop, calls=%fused_computation.134 | loop fusion | bytes 23068672 | tf_op jit(solution)/shard_map/slice | solution.py:130
  310.4 8.4 %copy.40 = bf16[2816,1024]{0,1:T(8,128)(2,1)} copy(bf16[2816,1024]{1,0:T(8,128)(2,1)} %get-tuple-element.65) | data formatting | bytes 11534336
  318.8 8.4 %copy.39 = bf16[2816,1024]{0,1:T(8,128)(2,1)} copy(bf16[2816,1024]{1,0:T(8,128)(2,1)} %get-tuple-element.66) | data formatting | bytes 11534336
  327.2 63.7 %while.11 = (s32[]{:T(128)}, bf16[4,256,4,64]{1,3,2,0:T(8,128)(2,1)S(1)}, bf16[4,2816,4,64]{1,3,2,0:T(8,128)(2,1)}, pred[11,256]{1,0:T(8,128)(4,1)}, bf16[4,256,...) while((s32[]{:T(128)}, ...), condition=%wide.wide.region_8.9_spmd, body=%wide.wide.region_5.8_spmd.sunk | while | flops 755501824 | bytes 26358620 | solution.py:58
  327.2 9.3 %fusion.134 = (f32[4,256]{1,0:T(4,128)S(1)}, f32[4,256,2816]{2,1,0:T(8,128)}) fusion(pred[2816]{0:T(1024)(128)(4,1)S(1)} %get-tuple-element.174, bf16[4,2816,4,64]{1,3,2,0:T(8,128)(2,1)} %get-tuple-element.173, s32[]{:T(128)S(6)} %copy.71, bf16[4,256,4,64]{1,3,2,0:T(8,128)(2,1)} %get-tuple-element.172), kind=kOutput, calls=%fused_computation.133.clone.clone.1 | convolution fusion | flops 380635904 | bytes 13115136 | tf_op jit(solution)/shard_map/while/body/eval_jaxpr/sub | solution.py:52
  336.5 6.6 %fusion.135 = bf16[4,256,4,64]{1,3,2,0:T(8,128)(2,1)S(1)} fusion(bf16[4,256,4,64]{1,3,2,0:T(8,128)(2,1)S(1)} %get-tuple-element.161, s32[]{:T(128)S(6)} %copy.71, f32[4,256,2816]{2,1,0:T(8,128)} %get-tuple-element.150, f32[4,256]{1,0:T(4,128)S(1)} %get-tuple-element.151, bf16[4,2816,4,64]{1,3,2,0:T(8,128)(2,1)} %get-tuple-element.170), kind=kOutput, calls=%fused_computation.21.clone.clone.1 | convolution fusion | flops 374865920 | bytes 13243392 | tf_op jit(solution)/shard_map/while/body/eval_jaxpr/hqk,khd->qhd/dot_general | solution.py:54
  343.2 9.3 %fusion.134 = (f32[4,256]{1,0:T(4,128)S(1)}, f32[4,256,2816]{2,1,0:T(8,128)}) fusion(pred[2816]{0:T(1024)(128)(4,1)S(1)} %get-tuple-element.174, bf16[4,2816,4,64]{1,3,2,0:T(8,128)(2,1)} %get-tuple-element.173, s32[]{:T(128)S(6)} %copy.71, bf16[4,256,4,64]{1,3,2,0:T(8,128)(2,1)} %get-tuple-element.172), kind=kOutput, calls=%fused_computation.133.clone.clone.1 | convolution fusion | flops 380635904 | bytes 13115136 | tf_op jit(solution)/shard_map/while/body/eval_jaxpr/sub | solution.py:52
  352.5 6.6 %fusion.135 = bf16[4,256,4,64]{1,3,2,0:T(8,128)(2,1)S(1)} fusion(bf16[4,256,4,64]{1,3,2,0:T(8,128)(2,1)S(1)} %get-tuple-element.161, s32[]{:T(128)S(6)} %copy.71, f32[4,256,2816]{2,1,0:T(8,128)} %get-tuple-element.150, f32[4,256]{1,0:T(4,128)S(1)} %get-tuple-element.151, bf16[4,2816,4,64]{1,3,2,0:T(8,128)(2,1)} %get-tuple-element.170), kind=kOutput, calls=%fused_computation.21.clone.clone.1 | convolution fusion | flops 374865920 | bytes 13243392 | tf_op jit(solution)/shard_map/while/body/eval_jaxpr/hqk,khd->qhd/dot_general | solution.py:54
  359.1 9.3 %fusion.134 = (f32[4,256]{1,0:T(4,128)S(1)}, f32[4,256,2816]{2,1,0:T(8,128)}) fusion(pred[2816]{0:T(1024)(128)(4,1)S(1)} %get-tuple-element.174, bf16[4,2816,4,64]{1,3,2,0:T(8,128)(2,1)} %get-tuple-element.173, s32[]{:T(128)S(6)} %copy.71, bf16[4,256,4,64]{1,3,2,0:T(8,128)(2,1)} %get-tuple-element.172), kind=kOutput, calls=%fused_computation.133.clone.clone.1 | convolution fusion | flops 380635904 | bytes 13115136 | tf_op jit(solution)/shard_map/while/body/eval_jaxpr/sub | solution.py:52
  368.4 6.6 %fusion.135 = bf16[4,256,4,64]{1,3,2,0:T(8,128)(2,1)S(1)} fusion(bf16[4,256,4,64]{1,3,2,0:T(8,128)(2,1)S(1)} %get-tuple-element.161, s32[]{:T(128)S(6)} %copy.71, f32[4,256,2816]{2,1,0:T(8,128)} %get-tuple-element.150, f32[4,256]{1,0:T(4,128)S(1)} %get-tuple-element.151, bf16[4,2816,4,64]{1,3,2,0:T(8,128)(2,1)} %get-tuple-element.170), kind=kOutput, calls=%fused_computation.21.clone.clone.1 | convolution fusion | flops 374865920 | bytes 13243392 | tf_op jit(solution)/shard_map/while/body/eval_jaxpr/hqk,khd->qhd/dot_general | solution.py:54
  375.1 9.3 %fusion.134 = (f32[4,256]{1,0:T(4,128)S(1)}, f32[4,256,2816]{2,1,0:T(8,128)}) fusion(pred[2816]{0:T(1024)(128)(4,1)S(1)} %get-tuple-element.174, bf16[4,2816,4,64]{1,3,2,0:T(8,128)(2,1)} %get-tuple-element.173, s32[]{:T(128)S(6)} %copy.71, bf16[4,256,4,64]{1,3,2,0:T(8,128)(2,1)} %get-tuple-element.172), kind=kOutput, calls=%fused_computation.133.clone.clone.1 | convolution fusion | flops 380635904 | bytes 13115136 | tf_op jit(solution)/shard_map/while/body/eval_jaxpr/sub | solution.py:52
  384.3 6.6 %fusion.135 = bf16[4,256,4,64]{1,3,2,0:T(8,128)(2,1)S(1)} fusion(bf16[4,256,4,64]{1,3,2,0:T(8,128)(2,1)S(1)} %get-tuple-element.161, s32[]{:T(128)S(6)} %copy.71, f32[4,256,2816]{2,1,0:T(8,128)} %get-tuple-element.150, f32[4,256]{1,0:T(4,128)S(1)} %get-tuple-element.151, bf16[4,2816,4,64]{1,3,2,0:T(8,128)(2,1)} %get-tuple-element.170), kind=kOutput, calls=%fused_computation.21.clone.clone.1 | convolution fusion | flops 374865920 | bytes 13243392 | tf_op jit(solution)/shard_map/while/body/eval_jaxpr/hqk,khd->qhd/dot_general | solution.py:54
  391.0 1.7 fusion.62
  (42 shorter events, 0.9 us)
Async XLA Ops:
  6.5 384.4 %copy-start = (bf16[1024,1024]{1,0:T(8,128)(2,1)S(1)}, bf16[1024,1024]{1,0:T(8,128)(2,1)}, u32[]{:S(2)}) copy-start(bf16[1024,1024]{1,0:T(8,128)(2,1)} %param.9) | copy-start | bytes 6291460
  6.5 10.6 %copy-start.6 = (s32[8,32,8]{1,2,0:T(8,128)S(1)}, s32[8,32,8]{1,2,0:T(8,128)}, u32[]{:S(2)}) copy-start(s32[8,32,8]{1,2,0:T(8,128)} %param.10) | copy-start | bytes 24580
  6.5 12.1 %copy-start.5 = (s32[8,8192]{1,0:T(8,128)S(1)}, s32[8,8192]{1,0:T(8,128)}, u32[]{:S(2)}) copy-start(s32[8,8192]{1,0:T(8,128)} %param.11) | copy-start | bytes 786436
  6.5 63.9 %all-gather.3.cloned.1.call-start = ((), (), s32[]{:S(2)}) async-start(), calls=%async_computation | async-start | bytes 9437184 | tf_op jit(solution)/shard_map/all_gather | solution.py:110
  11.4 1.2 copy-start.2
  13.8 277.0 %collective-permute-start.1 = (bf16[1,256,2048]{2,1,0:T(8,128)(2,1)S(1)}, bf16[1,256,2048]{2,1,0:T(8,128)(2,1)}, u32[]{:S(2)}, u32[]{:S(2)}) collective-permute-start(bf16[1,256,2048]{2,1,0:T(8,128)(2,1)S(1)} %get-tuple-element.67), channel_id=1, source_target_pairs={{1,0},{2,1},{3,2},{4,3},{5,4},{6,5},{7,6},{8,7},{9,8},{10,9},{11,1... | collective-permute-start | bytes 3145736 | tf_op jit(solution)/shard_map/ppermute | solution.py:22
  20.5 73.9 %copy-start.7 = (pred[11,256]{1,0:T(8,128)(4,1)}, pred[11,256]{1,0:T(8,128)(4,1)S(1)}, u32[]{:S(2)}) copy-start(pred[11,256]{1,0:T(8,128)(4,1)S(1)} %pad_add_fusion) | copy-start | bytes 8452
  70.5 16.9 %copy-start.1 = (bf16[2048,2048]{1,0:T(8,128)(2,1)S(1)}, bf16[2048,2048]{1,0:T(8,128)(2,1)}, u32[]{:S(2)}) copy-start(bf16[2048,2048]{1,0:T(8,128)(2,1)} %all-gather.3.cloned.1.call-done) | copy-start | bytes 25165828
  81.4 49.8 %collective-permute-start.2 = (bf16[2,256,2048]{2,0,1:T(2,128)(2,1)}, bf16[2,256,2048]{2,0,1:T(2,128)(2,1)}, u32[]{:S(2)}, u32[]{:S(2)}) collective-permute-start(bf16[2,256,2048]{2,0,1:T(2,128)(2,1)} %fusion.50), channel_id=1, source_target_pairs={{0,2},{1,3},{2,4},{3,5},{4,6},{5,7},{6,8},{7,9},{8,10},{9,11},{10,... | collective-permute-start | bytes 6291464 | tf_op jit(solution)/shard_map/ppermute | solution.py:32
  94.4 133.6 %collective-permute-start.3 = (bf16[2,256,2048]{2,0,1:T(2,128)(2,1)}, bf16[2,256,2048]{2,0,1:T(2,128)(2,1)}, u32[]{:S(2)}, u32[]{:S(2)}) collective-permute-start(bf16[2,256,2048]{2,0,1:T(2,128)(2,1)} %fusion.53), channel_id=1, source_target_pairs={{0,1},{1,2},{2,3},{3,4},{4,5},{5,6},{6,7},{7,8},{8,9},{9,10},{10,1... | collective-permute-start | bytes 6291464 | tf_op jit(solution)/shard_map/ppermute | solution.py:32
  104.9 162.0 %collective-permute-start.4 = (bf16[2,256,2048]{2,0,1:T(2,128)(2,1)}, bf16[2,256,2048]{2,0,1:T(2,128)(2,1)}, u32[]{:S(2)}, u32[]{:S(2)}) collective-permute-start(bf16[2,256,2048]{2,0,1:T(2,128)(2,1)} %fusion.56), channel_id=1, source_target_pairs={{1,0},{2,1},{3,2},{4,3},{5,4},{6,5},{7,6},{8,7},{9,8},{10,9},{11,1... | collective-permute-start | bytes 6291464 | tf_op jit(solution)/shard_map/ppermute | solution.py:32
  113.2 157.5 %collective-permute-start.5 = (bf16[2,256,2048]{2,0,1:T(2,128)(2,1)}, bf16[2,256,2048]{2,0,1:T(2,128)(2,1)S(1)}, u32[]{:S(2)}, u32[]{:S(2)}) collective-permute-start(bf16[2,256,2048]{2,0,1:T(2,128)(2,1)} %fusion.59), channel_id=1, source_target_pairs={{2,0},{3,1},{4,2},{5,3},{6,4},{7,5},{8,6},{9,7},{10,8},{11,9},{12,... | collective-permute-start | bytes 6291464 | tf_op jit(solution)/shard_map/ppermute | solution.py:32
  131.2 159.7 %collective-permute-start = (bf16[1,256,2048]{2,1,0:T(8,128)(2,1)S(1)}, bf16[1,256,2048]{2,1,0:T(8,128)(2,1)}, u32[]{:S(2)}, u32[]{:S(2)}) collective-permute-start(bf16[1,256,2048]{2,1,0:T(8,128)(2,1)S(1)} %get-tuple-element.67), channel_id=1, source_target_pairs={{0,1},{1,2},{2,3},{3,4},{4,5},{5,6},{6,7},{7,8},{8,9},{9,10},{10,1... | collective-permute-start | bytes 3145736 | tf_op jit(solution)/shard_map/ppermute | solution.py:20
  318.8 8.4 %copy-start.4 = (bf16[4,256,4,64]{1,3,2,0:T(8,128)(2,1)S(1)}, bf16[4,256,4,64]{1,3,2,0:T(8,128)(2,1)}, u32[]{:S(2)}) copy-start(bf16[4,256,4,64]{1,3,2,0:T(8,128)(2,1)} %custom-call.7) | copy-start | bytes 1572868
  327.2 63.7 %copy-start.3 = (bf16[1,256,1024]{2,1,0:T(8,128)(2,1)S(1)}, bf16[1,256,1024]{2,1,0:T(8,128)(2,1)}, u32[]{:S(2)}) copy-start(bf16[1,256,1024]{2,1,0:T(8,128)(2,1)} %param.7) | copy-start | bytes 1572868
Sparse Core Ops, SparseCore 0:
  14.0 56.4 all-gather.2
where the time goes:
time: 401 us; the launch traced here: 400 us
  starting transfers between devices  106 us (26%)
  matrix products  102 us (25%)
  waiting for transfers between devices  91.4 us (23%)
  local copies, waits for them, and re-layouts  66.8 us (17%)
  other arithmetic  19.1 us (5%)
  between operations  13.6 us (3%)
    ppermute x1, starting transfers between devices, with_halo(): lax.ppermute(tail, axis, [(i, (i + 1) % count) for i in range(ends)])  93 us
    all_gather x1, waiting for transfers between devices, body(): gathered = lax.all_gather(key_value[None], 'view', axis=0, tiled=True)  47.9 us
    ppermute x4, waiting for transfers between devices, from_behind(): return lax.ppermute(block, axis, route)  43.5 us
    unnamed x23, local copies, waits for them, and re-layouts  37.8 us
    sub x4, matrix products, per_group(): raised = jnp.exp(scores - row_top)  37 us
    dot_general x4, matrix products, offset_payload(): jnp.einsum('rw,wtc->rtc', picker, pick_from, preferred_element_type=jnp.f...  31.9 us
    dot_general x4, matrix products, per_group(): jnp.einsum('hqk,khd->qhd', attention, value_block, preferred_element_type...  26.6 us
    ppermute x4, starting transfers between devices, from_behind(): return lax.ppermute(block, axis, route)  12.1 us
  transfers between devices with their start and end apart: 7, of which 3 were waited for; matrix products, arithmetic and copies ran while one was open for 20% of the time, Pallas kernels for 0%

commit v1 on v0

v1 whole, which is shorter than its diff:
```python
import functools

import jax
import jax.numpy as jnp
from jax import lax
from jax.experimental import pallas as pl
from jax.experimental.pallas import tpu as pltpu
from jax.sharding import PartitionSpec as P

MESH = pl.DeviceIdType.MESH
HEAD_DIM = 64
REACH = 2
NEAR = 3
FAR = 4
BIG = -1e30
VALID = 64


def exchange_plan(chips):
    order = [0] + sorted(range(1, chips), key=lambda o: -min(o, chips - o))
    return order


def kernel(
    views, bands, table, lat, w_qkv, w_out, mask, out,
    w_buf, wo_buf, mask_buf, kv_send, q_send, kv_near, kv_far, q_buf, k_cat, v_cat,
    acc_buf, top_buf, o_send, o_buf,
    w_sem, wo_sem, mask_sem, kv_ssem, kv_rsem, up_ssem, up_rsem, down_ssem, down_rsem,
    up2_ssem, up2_rsem, down2_ssem, down2_rsem, q_ssem, q_rsem, o_ssem, o_rsem,
):
    tokens, width = lat.shape
    cols = width // views
    pair = 2 * cols
    chips = views // 2
    me = lax.axis_index("view")
    band = lax.axis_index("band")
    chip, core = me // 2, me % 2
    above, below = (band + 1) % bands, (band + bands - 1) % bands

    barrier = pltpu.get_barrier_semaphore()
    for off in range(1, views):
        pl.semaphore_signal(barrier, 1, device_id=((me + off) % views, band), device_id_type=MESH)
    for other in (above, below):
        pl.semaphore_signal(barrier, 1, device_id=(me, other), device_id_type=MESH)

    order = exchange_plan(chips)
    loads = []
    for n, off in enumerate(order):
        there = (chip + off) % chips
        for part in (1, 2, 0):
            load = pltpu.make_async_copy(
                w_qkv.at[:, pl.ds(pl.multiple_of(part * width + there * pair, pair), pair)],
                w_buf.at[n, part],
                w_sem.at[n, part],
            )
            load.start()
            loads.append(load)
    masks = []
    for n, d in enumerate((-1, 0, 1, -2, 2)):
        at = jnp.clip(band + d, 0, bands - 1)
        load = pltpu.make_async_copy(
            mask.at[:, pl.ds(pl.multiple_of(at * tokens, tokens), tokens)],
            mask_buf.at[pl.ds(n * views, views)],
            mask_sem.at[n],
        )
        load.start()
        masks.append(load)
    wo_load = pltpu.make_async_copy(w_out, wo_buf, wo_sem)
    wo_load.start()

    def copy(src, dst, ssem, rsem, view, at):
        return pltpu.make_async_remote_copy(
            src_ref=src, dst_ref=dst, send_sem=ssem, recv_sem=rsem,
            device_id=(view, at), device_id_type=MESH,
        )

    def kv_to(view):
        return copy(kv_send.at[view], kv_near.at[views + me], kv_ssem.at[view], kv_rsem.at[me], view, band)

    def q_to(view):
        return copy(q_send.at[view], q_buf.at[me], q_ssem.at[view], q_rsem.at[me], view, band)

    def kv_from(view):
        return copy(kv_send.at[view], kv_near.at[views + view], kv_ssem.at[view], kv_rsem.at[view], view, band)

    def q_from(view):
        return copy(q_send.at[view], q_buf.at[view], q_ssem.at[view], q_rsem.at[view], view, band)

    def up(view):
        return copy(kv_near.at[views + view], kv_near.at[view], up_ssem.at[view], up_rsem.at[view], me, above)

    def down(view):
        return copy(kv_near.at[views + view], kv_near.at[2 * views + view], down_ssem.at[view], down_rsem.at[view], me, below)

    def up2(view):
        return copy(kv_near.at[view], kv_far.at[view], up2_ssem.at[view], up2_rsem.at[view], me, above)

    def down2(view):
        return copy(kv_near.at[2 * views + view], kv_far.at[views + view], down2_ssem.at[view], down2_rsem.at[view], me, below)

    row = lat[...]
    scale = HEAD_DIM**-0.5

    def project(n, part):
        loads[3 * n + {1: 0, 2: 1, 0: 2}[part]].wait()
        return jnp.dot(row, w_buf[n, part], preferred_element_type=jnp.float32).astype(jnp.bfloat16)

    def put_pair(there, part, value):
        for c in range(2):
            kv_send[2 * there + c, part] = value[:, c * cols : (c + 1) * cols]

    for n, off in enumerate(order):
        there = (chip + off) % chips
        put_pair(there, 0, project(n, 1))
        put_pair(there, 1, project(n, 2))
        if n == 0:
            kv_near[views + me] = kv_send[me]
            pl.semaphore_wait(barrier, views + 1)
            up(me).start()
            down(me).start()
            kv_to(2 * chip + 1 - core).start()
        else:
            for c in range(2):
                kv_to(2 * there + c).start()
        queries = project(n, 0) * jnp.bfloat16(scale)
        for c in range(2):
            q_send[2 * there + c] = queries[:, c * cols : (c + 1) * cols]
        if n == 0:
            q_buf[me] = q_send[me]

    others = [2 * chip + 1 - core]
    for off in sorted(range(1, chips), key=lambda o: min(o, chips - o)):
        others += [2 * ((chip + off) % chips) + c for c in range(2)]
    for view in reversed(others):
        q_to(view).start()
    for view in others:
        kv_from(view).wait_recv()
        up(view).start()
        down(view).start()
    for view in [me, *others]:
        up(view).wait_recv()
        up2(view).start()
        down(view).wait_recv()
        down2(view).start()
    for load in masks:
        load.wait()
    for view in others:
        q_from(view).wait_recv()

    v_cat[:, cols:] = jnp.ones((v_cat.shape[0], cols), jnp.bfloat16)
    lane = lax.broadcasted_iota(jnp.int32, (tokens, cols), 1)

    def bias_row(index, valid):
        seen = mask_buf[pl.ds(index, 1), :] * valid
        return jnp.where(seen > 0, 0.0, BIG)

    def attend(view, bias, keys):
        q = q_buf[view]
        results = []
        for h in range(2):
            mine = lane // HEAD_DIM == h
            qh = jnp.where(mine, q, jnp.zeros_like(q))
            s = lax.dot_general(
                qh, k_cat[:keys], (((1,), (1,)), ((), ())), preferred_element_type=jnp.float32
            )
            s = s + bias
            top = jnp.max(s, axis=1, keepdims=True)
            p = jnp.exp(s - top).astype(jnp.bfloat16)
            results.append((jnp.dot(p, v_cat[:keys], preferred_element_type=jnp.float32), top))
        return results

    def near_step(i, carry):
        view = (me + 1 + i) % views
        rows = []
        up_ok = jnp.where(band > 0, 1, 0)
        down_ok = jnp.where(band < bands - 1, 1, 0)
        spots = [(views + view, 1), (view, up_ok), (2 * views + view, down_ok)]
        for r in range(NEAR):
            code = table[view, r]
            spots.append((code % VALID, code // VALID))
        for n, (index, valid) in enumerate(spots):
            k_cat[n * tokens : (n + 1) * tokens] = kv_near[index, 0]
            v_cat[n * tokens : (n + 1) * tokens, :cols] = kv_near[index, 1]
            rows.append(bias_row(index, valid))
        for h, (acc, top) in enumerate(attend(view, jnp.concatenate(rows, axis=1), (3 + NEAR) * tokens)):
            acc_buf[i, h] = acc
            top_buf[i, h] = jnp.broadcast_to(top, (tokens, cols))
        return carry

    lax.fori_loop(0, views, near_step, 0)

    for view in [me, *others]:
        up2(view).wait_recv()
        down2(view).wait_recv()

    def far_step(i, carry):
        view = (me + 1 + i) % views
        rows = []
        for n in range(FAR):
            code = table[view, NEAR + n]
            index, valid = code % VALID, code // VALID
            near_index = jnp.minimum(index, 3 * views - 1)
            far_index = jnp.maximum(index - 3 * views, 0)
            is_near = index < 3 * views
            k_cat[n * tokens : (n + 1) * tokens] = jnp.where(is_near, kv_near[near_index, 0], kv_far[far_index, 0])
            v_cat[n * tokens : (n + 1) * tokens, :cols] = jnp.where(
                is_near, kv_near[near_index, 1], kv_far[far_index, 1]
            )
            rows.append(bias_row(index, valid))
        blends = []
        for h, (acc, top) in enumerate(attend(view, jnp.concatenate(rows, axis=1), FAR * tokens)):
            old = top_buf[i, h][:, :1]
            new = jnp.maximum(old, top)
            total = acc_buf[i, h] * jnp.exp(old - new) + acc * jnp.exp(top - new)
            blends.append(total[:, :cols] / total[:, cols:])
        blend = jnp.where(lane < HEAD_DIM, blends[0], blends[1]).astype(jnp.bfloat16)
        o_send[view] = blend

        @pl.when(i < views - 1)
        def _():
            copy(o_send.at[view], o_buf.at[me], o_ssem.at[view], o_rsem.at[me], view, band).start()

        return carry

    lax.fori_loop(0, views, far_step, 0)
    o_buf[me] = o_send[me]
    wo_load.wait()
    for view in others:
        copy(o_send.at[view], o_buf.at[view], o_ssem.at[view], o_rsem.at[view], view, band).wait_recv()
    total = row.astype(jnp.float32)
    for c in range(chips):
        both = jnp.concatenate([o_buf[2 * c], o_buf[2 * c + 1]], axis=1)
        total = total + jnp.dot(both, wo_buf[c * pair : (c + 1) * pair], preferred_element_type=jnp.float32)
    out[...] = total

    for view in others:
        kv_to(view).wait_send()
        q_to(view).wait_send()
        copy(o_send.at[view], o_buf.at[me], o_ssem.at[view], o_rsem.at[me], view, band).wait_send()
    for view in [me, *others]:
        for way in (up, down, up2, down2):
            way(view).wait_send()


def epipolar_table(epipolar_bands, band, views):
    listed = lax.dynamic_index_in_dim(epipolar_bands, band, axis=1, keepdims=False)
    far = listed - band
    numbers = jnp.arange(views, dtype=jnp.int32)
    own = numbers[:, None] == numbers[None, :]
    present = (listed >= 0) & ~own
    slot = jnp.where(far == -2, 3, jnp.where(far == 2, 4, jnp.clip(far, -1, 1) + 1))
    code = jnp.where(present, slot * views + numbers[None, :] + VALID, views + numbers[None, :])
    key = jnp.where(own, REACH + 1, jnp.where(present, jnp.abs(far), 0)) * views + numbers[None, :]
    rank = jnp.sum((key[:, None, :] < key[:, :, None]).astype(jnp.int32), axis=2)
    return jnp.sum(jnp.where(rank[:, :, None] == numbers[None, None, :], code[:, :, None], 0), axis=1)


def body(latents, w_qkv, w_out, epipolar_bands, object_token_mask):
    views = lax.axis_size("view")
    bands = lax.axis_size("band")
    tokens, width = latents.shape[1:]
    cols = width // views
    table = epipolar_table(epipolar_bands, lax.axis_index("band"), views)
    bf16, f32 = jnp.bfloat16, jnp.float32
    dma = pltpu.SemaphoreType.DMA
    vmem = pl.BlockSpec(memory_space=pltpu.VMEM)
    hbm = pl.BlockSpec(memory_space=pltpu.HBM)
    updated = pl.pallas_call(
        functools.partial(kernel, views, bands),
        out_shape=jax.ShapeDtypeStruct((tokens, width), f32),
        in_specs=[pl.BlockSpec(memory_space=pltpu.SMEM), vmem, hbm, hbm, hbm],
        out_specs=vmem,
        scratch_shapes=[
            pltpu.VMEM((views // 2, 3, width, 2 * cols), bf16),
            pltpu.VMEM((width, width), bf16),
            pltpu.VMEM((5 * views, tokens), jnp.int32),
            pltpu.VMEM((views, 2, tokens, cols), bf16),
            pltpu.VMEM((views, tokens, cols), bf16),
            pltpu.VMEM((3 * views, 2, tokens, cols), bf16),
            pltpu.VMEM((2 * views, 2, tokens, cols), bf16),
            pltpu.VMEM((views, tokens, cols), bf16),
            pltpu.VMEM(((3 + NEAR) * tokens, cols), bf16),
            pltpu.VMEM(((3 + NEAR) * tokens, 2 * cols), bf16),
            pltpu.VMEM((views, 2, tokens, 2 * cols), f32),
            pltpu.VMEM((views, 2, tokens, cols), f32),
            pltpu.VMEM((views, tokens, cols), bf16),
            pltpu.VMEM((views, tokens, cols), bf16),
            dma((views // 2, 3)),
            dma,
            dma((5,)),
            *[dma((views,)) for _ in range(14)],
        ],
        compiler_params=pltpu.CompilerParams(
            collective_id=0, has_side_effects=True, vmem_limit_bytes=60 * 2**20
        ),
    )(table, latents[0], w_qkv, w_out, object_token_mask)
    return updated[None]


def solution(mesh):
    placed = (P("view", "band", None), P(), P(), P(), P())
    return jax.shard_map(
        body, mesh=mesh, in_specs=placed, out_specs=P("view", "band", None), check_vma=False
    )
```

time: 401 us -> 84 us (0.21)
  starting transfers between devices: 106 us -> 0 us
  matrix products: 102 us -> 0 us
  waiting for transfers between devices: 91.4 us -> 0 us
  Pallas kernels: 0 us -> 79.5 us
  local copies, waits for them, and re-layouts: 66.8 us -> 3.25 us
  other arithmetic: 19.1 us -> 1 us
  between operations: 13.6 us -> 0.02 us
    ppermute x6 -> x0, starting transfers between devices: 106 us -> none  [the longest x1 93 us: with_halo(): lax.ppermute(tail, axis, [(i, (i + 1) % count) for i in range(ends)])]
    pallas_call x0 -> x1, Pallas kernels: none -> 79.5 us  [body(): pl.pallas_call(functools.partial(kernel, views, bands), out_shape=jax.Sha...]
    dot_general x10 -> x0, matrix products: 65.1 us -> none  [the longest x4 31.9 us: offset_payload(): jnp.einsum('rw,wtc->rtc', picker, pick_from, preferred_element_type=jnp.f...]
    all_gather x1 -> x0, waiting for transfers between devices: 47.9 us -> none  [body(): gathered = lax.all_gather(key_value[None], 'view', axis=0, tiled=True)]
    ppermute x6 -> x0, waiting for transfers between devices: 43.5 us -> none  [the longest x4 43.5 us: from_behind(): return lax.ppermute(block, axis, route)]
    sub x4 -> x0, matrix products: 37 us -> none  [per_group(): raised = jnp.exp(scores - row_top)]
    unnamed x23 -> x4, local copies, waits for them, and re-layouts: 37.8 us -> 3.18 us
    slice x3 -> x0, local copies, waits for them, and re-layouts: 14 us -> none  [the longest x1 10 us: body(): flattened[:, :width]]
  transfers between devices with their start and end apart: 7 -> 0, of which waited for: 3 -> 0; matrix products, arithmetic and copies ran while one was open for 20% -> 0% of each run, Pallas kernels for 0% -> 0%
where the time goes in v1:
time: 84 us; the launch traced here: 83.8 us
  Pallas kernels  79.5 us (95%)
  local copies, waits for them, and re-layouts  3.25 us (4%)
  other arithmetic  1 us (1%)
    pallas_call x1, Pallas kernels, body(): pl.pallas_call(functools.partial(kernel, views, bands), out_shape=jax.Sha...  79.5 us
    unnamed x4, local copies, waits for them, and re-layouts  3.18 us

profile of v1, /device:TPU:1, one launch (start us, length us, event | category | flops | bytes accessed | tf_op | source)
XLA Modules:
  0.0 83.8 jit_solution(8475096475145548383)
XLA Ops:
  0.0 0.0 copy-start
  0.0 0.8 copy-done
  0.8 0.1 constant_dynamic-slice_fusion
  0.8 0.1 copy.8
  1.0 0.3 convert_reduce_fusion
  1.3 0.7 select_reduce_fusion.table
  2.0 79.5 %shard_map.55 = f32[256,1024]{1,0:T(8,128)} custom-call(s32[8,8]{1,0:T(8,128)} %select_reduce_fusion.table, bf16[256,1024]{1,0:T(8,128)(2,1)} %bitcast.25, bf16[1024,3072]{1,0:T(8,128)(2,1)} %w_qkv.1, bf16[1024,1024]{1,0:T(8,128)(2,1)} %w_out.1, s32[8,8192]{1,0:T(8,128)} %mask.1), custom_call_target="tpu_custom_call" | custom-call | tf_op jit(solution)/shard_map/pallas_call | solution.py:268
  81.5 2.3 %copy.10 = f32[1,256,1024]{2,1,0:T(8,128)} copy(f32[1,256,1024]{2,1,0:T(8,128)} %bitcast.24) | data formatting | bytes 2097152
  (3 shorter events, 0.0 us)
Async XLA Ops:
  0.0 0.8 copy-start

commit v2 on v1

--- a/solution.py
+++ b/solution.py
@@ -12,6 +12,7 @@
 REACH = 2
 NEAR = 3
 FAR = 4
+RING = 4
 BIG = -1e30
 VALID = 64
 
@@ -26,7 +27,7 @@
     w_buf, wo_buf, mask_buf, kv_send, q_send, kv_near, kv_far, q_buf, k_cat, v_cat,
     acc_buf, top_buf, o_send, o_buf,
     w_sem, wo_sem, mask_sem, kv_ssem, kv_rsem, up_ssem, up_rsem, down_ssem, down_rsem,
-    up2_ssem, up2_rsem, down2_ssem, down2_rsem, q_ssem, q_rsem, o_ssem, o_rsem,
+    hop_ssem, cross_ssem, far_rsem, q_ssem, q_rsem, o_ssem, o_rsem,
 ):
     tokens, width = lat.shape
     cols = width // views
@@ -36,11 +37,16 @@
     band = lax.axis_index("band")
     chip, core = me // 2, me % 2
     above, below = (band + 1) % bands, (band + bands - 1) % bands
+    place = band % RING
+    edge, upper, odd = ((place + 1) // 2 + 1) % 2, place // 2, place % 2
+    first, last = edge * (1 - upper), edge * upper
+    over, under = (band + RING) % bands, (band + bands - RING) % bands
+    across = (band + bands + (3 - 2 * place)) % bands
 
     barrier = pltpu.get_barrier_semaphore()
     for off in range(1, views):
         pl.semaphore_signal(barrier, 1, device_id=((me + off) % views, band), device_id_type=MESH)
-    for other in (above, below):
+    for other in (above, below, over, under, across):
         pl.semaphore_signal(barrier, 1, device_id=(me, other), device_id_type=MESH)
 
     order = exchange_plan(chips)
@@ -92,11 +98,29 @@
     def down(view):
         return copy(kv_near.at[views + view], kv_near.at[2 * views + view], down_ssem.at[view], down_rsem.at[view], me, below)
 
-    def up2(view):
-        return copy(kv_near.at[view], kv_far.at[view], up2_ssem.at[view], up2_rsem.at[view], me, above)
-
-    def down2(view):
-        return copy(kv_near.at[2 * views + view], kv_far.at[views + view], down2_ssem.at[view], down2_rsem.at[view], me, below)
+    def hop_down(view):
+        return copy(
+            kv_near.at[2 * views + view, edge], kv_far.at[(1 - first) * views + view, edge], hop_ssem.at[0, view],
+            far_rsem.at[1 - first, edge, view], me, (band + bands - 1 + RING * first) % bands,
+        )
+
+    def hop_up(view):
+        return copy(
+            kv_near.at[view, edge], kv_far.at[last * views + view, edge], hop_ssem.at[1, view],
+            far_rsem.at[last, edge, view], me, (band + bands + 1 - RING * last) % bands,
+        )
+
+    def cross(view, half):
+        back = upper if half == 0 else odd
+        return copy(
+            kv_far.at[(1 - back) * views + view, half], kv_far.at[back * views + view, half], cross_ssem.at[half, view],
+            far_rsem.at[back, half, view], me, (band + bands + RING * (1 - 2 * back)) % bands,
+        )
+
+    def hop_arrival(view, half):
+        back = upper if half == 0 else odd
+        at = kv_far.at[(1 - back) * views + view, half]
+        return copy(at, at, cross_ssem.at[half, view], far_rsem.at[1 - back, half, view], me, above)
 
     row = lat[...]
     scale = HEAD_DIM**-0.5
@@ -107,7 +131,10 @@
 
     def put_pair(there, part, value):
         for c in range(2):
-            kv_send[2 * there + c, part] = value[:, c * cols : (c + 1) * cols]
+            for half in range(2):
+                kv_send[2 * there + c, half, part] = value[
+                    half * tokens // 2 : (half + 1) * tokens // 2, c * cols : (c + 1) * cols
+                ]
 
     for n, off in enumerate(order):
         there = (chip + off) % chips
@@ -115,7 +142,7 @@
         put_pair(there, 1, project(n, 2))
         if n == 0:
             kv_near[views + me] = kv_send[me]
-            pl.semaphore_wait(barrier, views + 1)
+            pl.semaphore_wait(barrier, views + 4)
             up(me).start()
             down(me).start()
             kv_to(2 * chip + 1 - core).start()
@@ -133,15 +160,25 @@
         others += [2 * ((chip + off) % chips) + c for c in range(2)]
     for view in reversed(others):
         q_to(view).start()
-    for view in others:
+
+    def to_neighbours(view):
         kv_from(view).wait_recv()
         up(view).start()
         down(view).start()
-    for view in [me, *others]:
+
+    def hop_on(view):
         up(view).wait_recv()
-        up2(view).start()
+        hop_up(view).start()
         down(view).wait_recv()
-        down2(view).start()
+        hop_down(view).start()
+
+    to_neighbours(others[0])
+    for view in (me, others[0]):
+        hop_on(view)
+    for view in others[1:]:
+        to_neighbours(view)
+    for view in others[1:]:
+        hop_on(view)
     for load in masks:
         load.wait()
     for view in others:
@@ -179,19 +216,26 @@
             code = table[view, r]
             spots.append((code % VALID, code // VALID))
         for n, (index, valid) in enumerate(spots):
-            k_cat[n * tokens : (n + 1) * tokens] = kv_near[index, 0]
-            v_cat[n * tokens : (n + 1) * tokens, :cols] = kv_near[index, 1]
+            for half in range(2):
+                at = pl.ds(n * tokens + half * tokens // 2, tokens // 2)
+                k_cat[at] = kv_near[index, half, 0]
+                v_cat[at, :cols] = kv_near[index, half, 1]
             rows.append(bias_row(index, valid))
         for h, (acc, top) in enumerate(attend(view, jnp.concatenate(rows, axis=1), (3 + NEAR) * tokens)):
             acc_buf[i, h] = acc
             top_buf[i, h] = jnp.broadcast_to(top, (tokens, cols))
+        step = i // 2
+        sent = 2 * ((chip + step + step // 2 - 2 * (step // 3)) % chips) + (core + i) % 2
+        for half in range(2):
+            hop_arrival(sent, half).wait_recv()
+            cross(sent, half).start()
         return carry
 
     lax.fori_loop(0, views, near_step, 0)
 
     for view in [me, *others]:
-        up2(view).wait_recv()
-        down2(view).wait_recv()
+        for half in range(2):
+            cross(view, half).wait_recv()
 
     def far_step(i, carry):
         view = (me + 1 + i) % views
@@ -202,10 +246,10 @@
             near_index = jnp.minimum(index, 3 * views - 1)
             far_index = jnp.maximum(index - 3 * views, 0)
             is_near = index < 3 * views
-            k_cat[n * tokens : (n + 1) * tokens] = jnp.where(is_near, kv_near[near_index, 0], kv_far[far_index, 0])
-            v_cat[n * tokens : (n + 1) * tokens, :cols] = jnp.where(
-                is_near, kv_near[near_index, 1], kv_far[far_index, 1]
-            )
+            for half in range(2):
+                at = pl.ds(n * tokens + half * tokens // 2, tokens // 2)
+                k_cat[at] = jnp.where(is_near, kv_near[near_index, half, 0], kv_far[far_index, half, 0])
+                v_cat[at, :cols] = jnp.where(is_near, kv_near[near_index, half, 1], kv_far[far_index, half, 1])
             rows.append(bias_row(index, valid))
         blends = []
         for h, (acc, top) in enumerate(attend(view, jnp.concatenate(rows, axis=1), FAR * tokens)):
@@ -238,8 +282,10 @@
         q_to(view).wait_send()
         copy(o_send.at[view], o_buf.at[me], o_ssem.at[view], o_rsem.at[me], view, band).wait_send()
     for view in [me, *others]:
-        for way in (up, down, up2, down2):
+        for way in (up, down, hop_up, hop_down):
             way(view).wait_send()
+        for half in range(2):
+            cross(view, half).wait_send()
 
 
 def epipolar_table(epipolar_bands, band, views):
@@ -274,10 +320,10 @@
             pltpu.VMEM((views // 2, 3, width, 2 * cols), bf16),
             pltpu.VMEM((width, width), bf16),
             pltpu.VMEM((5 * views, tokens), jnp.int32),
-            pltpu.VMEM((views, 2, tokens, cols), bf16),
+            pltpu.VMEM((views, 2, 2, tokens // 2, cols), bf16),
             pltpu.VMEM((views, tokens, cols), bf16),
-            pltpu.VMEM((3 * views, 2, tokens, cols), bf16),
-            pltpu.VMEM((2 * views, 2, tokens, cols), bf16),
+            pltpu.VMEM((3 * views, 2, 2, tokens // 2, cols), bf16),
+            pltpu.VMEM((2 * views, 2, 2, tokens // 2, cols), bf16),
             pltpu.VMEM((views, tokens, cols), bf16),
             pltpu.VMEM(((3 + NEAR) * tokens, cols), bf16),
             pltpu.VMEM(((3 + NEAR) * tokens, 2 * cols), bf16),
@@ -288,7 +334,11 @@
             dma((views // 2, 3)),
             dma,
             dma((5,)),
-            *[dma((views,)) for _ in range(14)],
+            *[dma((views,)) for _ in range(6)],
+            dma((2, views)),
+            dma((2, views)),
+            dma((2, 2, views)),
+            *[dma((views,)) for _ in range(4)],
         ],
         compiler_params=pltpu.CompilerParams(
             collective_id=0, has_side_effects=True, vmem_limit_bytes=60 * 2**20

time: 84 us -> 86.4 us (1.029)
  Pallas kernels: 79.5 us -> 82 us
    pallas_call x1, Pallas kernels: 79.5 us -> 82 us  [body(): pl.pallas_call(functools.partial(kernel, views, bands), out_shape=jax.Sha...]
where the time goes in v2:
time: 86.4 us; the launch traced here: 86.2 us
  Pallas kernels  82 us (95%)
  local copies, waits for them, and re-layouts  3.25 us (4%)
  other arithmetic  1 us (1%)
    pallas_call x1, Pallas kernels, body(): pl.pallas_call(functools.partial(kernel, views, bands), out_shape=jax.Sha...  82 us
    unnamed x4, local copies, waits for them, and re-layouts  3.18 us

profile of v2, /device:TPU:1, one launch (start us, length us, event | category | flops | bytes accessed | tf_op | source)
XLA Modules:
  0.0 86.2 jit_solution(15991036677369422286)
XLA Ops:
  0.0 0.0 copy-start
  0.0 0.8 copy-done
  0.8 0.1 constant_dynamic-slice_fusion
  0.8 0.1 copy.8
  1.0 0.3 convert_reduce_fusion
  1.3 0.7 select_reduce_fusion.table
  2.0 82.0 %shard_map.55 = f32[256,1024]{1,0:T(8,128)} custom-call(s32[8,8]{1,0:T(8,128)} %select_reduce_fusion.table, bf16[256,1024]{1,0:T(8,128)(2,1)} %bitcast.25, bf16[1024,3072]{1,0:T(8,128)(2,1)} %w_qkv.1, bf16[1024,1024]{1,0:T(8,128)(2,1)} %w_out.1, s32[8,8192]{1,0:T(8,128)} %mask.1), custom_call_target="tpu_custom_call" | custom-call | tf_op jit(solution)/shard_map/pallas_call | solution.py:314
  83.9 2.3 %copy.10 = f32[1,256,1024]{2,1,0:T(8,128)} copy(f32[1,256,1024]{2,1,0:T(8,128)} %bitcast.24) | data formatting | bytes 2097152
  (3 shorter events, 0.0 us)
Async XLA Ops:
  0.0 0.8 copy-start

commit v3 on v1

v3 whole, which is shorter than its diff:
```python
import functools
import itertools

import jax
import jax.numpy as jnp
from jax import lax
from jax.experimental import pallas as pl
from jax.experimental.pallas import tpu as pltpu
from jax.sharding import PartitionSpec as P

MESH = pl.DeviceIdType.MESH
HEAD_DIM = 64
RING = 4
LISTED = 7
HARD = 3
EASY = 5
LAG = 4
BIG = -1e30
VALID = 64


def kernel(
    views, bands, table, lat, w_qkv, w_out, mask, out,
    w_buf, wo_buf, mask_buf, kv_send, q_send, kv_near, kv_far, q_buf, cat,
    acc_buf, top_buf, o_send, o_buf,
    w_sem, wo_sem, mask_sem, kv_ssem, kv_rsem, q_ssem, q_rsem, halo_ssem, halo_rsem, cross_ssem, cross_rsem,
    o_ssem, o_rsem,
):
    tokens, width = lat.shape
    part_rows = tokens // 2
    cols = width // views
    wide = 2 * cols
    chips = views // 2
    me = lax.axis_index("view")
    band = lax.axis_index("band")
    chip, core = me // 2, me % 2
    place = band % RING
    upper, odd = place // 2, place % 2
    head = (odd + upper) % 2
    base = band - odd
    partner = band + 1 - 2 * odd
    across = band + 3 - 2 * place
    over, under = (band + RING) % bands, (band + bands - RING) % bands
    beyond = (band + bands + RING * (1 - 2 * upper)) % bands

    def visit(step):
        near = step // 2 % chips
        return 2 * ((chip + near + near // 2 - 2 * (near // 3)) % chips) + (core + step) % 2

    loads = {}

    def fetch(part, n):
        there = visit(2 * n) // 2
        load = pltpu.make_async_copy(
            w_qkv.at[:, pl.ds(pl.multiple_of(part * width + there * wide, wide), wide)],
            w_buf.at[n, part],
            w_sem.at[n, part],
        )
        load.start()
        loads[n, part] = load

    for n, part in itertools.product(range(chips), (1, 2)):
        fetch(part, n)

    barrier = pltpu.get_barrier_semaphore()
    for off in range(1, views):
        for row in (band, partner):
            pl.semaphore_signal(barrier, 1, device_id=((me + off) % views, row), device_id_type=MESH)
    for row in (partner, across, over, under):
        pl.semaphore_signal(barrier, 1, device_id=(me, row), device_id_type=MESH)

    for n in range(chips):
        fetch(0, n)
    masks = []
    side = 2 - 4 * upper
    for group, shift in enumerate((0, side, -side)):
        for j in range(2):
            at = jnp.clip(base + shift + j, 0, bands - 1)
            load = pltpu.make_async_copy(
                mask.at[:, pl.ds(pl.multiple_of(at * tokens, tokens), tokens)],
                mask_buf.at[pl.ds((2 * group + j) * views, views)],
                mask_sem.at[2 * group + j],
            )
            load.start()
            masks.append(load)
    wo_load = pltpu.make_async_copy(w_out, wo_buf, wo_sem)
    wo_load.start()

    def copy(src, dst, ssem, rsem, view, at):
        return pltpu.make_async_remote_copy(
            src_ref=src, dst_ref=dst, send_sem=ssem, recv_sem=rsem,
            device_id=(view, at), device_id_type=MESH,
        )

    def kv_to(view, theirs):
        h = (head + theirs) % 2
        return copy(
            kv_send.at[view, h], kv_near.at[odd, me], kv_ssem.at[view, h], kv_rsem.at[odd, me],
            view, partner if theirs else band,
        )

    def q_to(view, theirs):
        h = (head + theirs) % 2
        return copy(
            q_send.at[view, h], q_buf.at[odd, me], q_ssem.at[view, h], q_rsem.at[odd, me],
            view, partner if theirs else band,
        )

    def kv_from(view, theirs):
        j = (odd + theirs) % 2
        at = kv_near.at[j, view]
        return copy(at, at, kv_ssem.at[view, 0], kv_rsem.at[j, view], me, partner)

    def q_from(view, theirs):
        j = (odd + theirs) % 2
        at = q_buf.at[j, view]
        return copy(at, at, q_ssem.at[view, 0], q_rsem.at[j, view], me, partner)

    def halo(view):
        return copy(
            kv_near.at[pl.ds(0, 2), view], kv_near.at[pl.ds(2, 2), view], halo_ssem.at[view], halo_rsem.at[view],
            me, across,
        )

    def cross(view):
        return copy(
            kv_near.at[pl.ds(2, 2), view], kv_far.at[pl.ds(0, 2), view], cross_ssem.at[view], cross_rsem.at[view],
            me, beyond,
        )

    def o_to(view, j):
        return copy(
            o_send.at[j, view], o_buf.at[2 * me + head], o_ssem.at[j, view], o_rsem.at[2 * me + head], view, base + j
        )

    def o_from(view, theirs):
        slot = 2 * view + (head + theirs) % 2
        at = o_buf.at[slot]
        return copy(at, at, o_ssem.at[0, view], o_rsem.at[slot], me, partner)

    row = lat[...]
    scale = HEAD_DIM**-0.5
    low = lax.broadcasted_iota(jnp.int32, (tokens, cols), 1) < HEAD_DIM
    low_part = lax.broadcasted_iota(jnp.int32, (part_rows, cols), 1) < HEAD_DIM

    def turn(x):
        return pltpu.roll(x, HEAD_DIM, 1)

    def project(n, part):
        loads[n, part].wait()
        return jnp.dot(row, w_buf[n, part], preferred_element_type=jnp.float32)

    others = [visit(step) for step in range(1, views)]

    for n in range(chips):
        there = visit(2 * n) // 2
        keys, values = project(n, 1), project(n, 2)
        for c in range(2):
            k = keys[:, c * cols : (c + 1) * cols]
            v = values[:, c * cols : (c + 1) * cols]
            kv_send[2 * there + c, 0] = jnp.where(low, k, turn(v)).astype(jnp.bfloat16)
            kv_send[2 * there + c, 1] = jnp.where(low, turn(k), v).astype(jnp.bfloat16)
        if n == 0:
            kv_near[odd, me] = kv_send[me, head]
            pl.semaphore_wait(barrier, 2 * views + 2)
            kv_to(me, 1).start()
            for theirs in range(2):
                kv_to(2 * chip + 1 - core, theirs).start()
        else:
            for c, theirs in itertools.product(range(2), range(2)):
                kv_to(2 * there + c, theirs).start()
    for n in range(chips):
        there = visit(2 * n) // 2
        queries = project(n, 0) * scale
        for c in range(2):
            first = queries[:part_rows, c * cols : (c + 1) * cols]
            second = queries[part_rows:, c * cols : (c + 1) * cols]
            q_send[2 * there + c, 0] = jnp.where(low_part, first, turn(second)).astype(jnp.bfloat16)
            q_send[2 * there + c, 1] = jnp.where(low_part, turn(first), second).astype(jnp.bfloat16)
        if n == 0:
            q_buf[odd, me] = q_send[me, head]
            q_to(me, 1).start()
            for theirs in range(2):
                q_to(2 * chip + 1 - core, theirs).start()
        else:
            for c, theirs in itertools.product(range(2), range(2)):
                q_to(2 * there + c, theirs).start()

    for load in masks:
        load.wait()
    cat[:, cols:] = jnp.ones((cat.shape[0], cols), jnp.bfloat16)

    def bias_row(index, valid):
        seen = mask_buf[pl.ds(index, 1), :] * valid
        return jnp.where(seen > 0, 0.0, BIG)

    def query(j, view):
        both = q_buf[j, view].astype(jnp.float32)
        rows = jnp.concatenate([jnp.where(low_part, both, 0.0), jnp.where(low_part, turn(both), 0.0)], axis=0)
        return rows.astype(jnp.bfloat16)

    def attend(q, rows, count):
        keys = count * tokens
        s = lax.dot_general(
            q, cat[:keys, :cols], (((1,), (1,)), ((), ())), preferred_element_type=jnp.float32
        )
        s = s + jnp.concatenate(rows, axis=1)
        top = jnp.max(s, axis=1, keepdims=True)
        p = jnp.exp(s - top).astype(jnp.bfloat16)
        return jnp.dot(p, cat[:keys], preferred_element_type=jnp.float32), top

    def store(j, view, acc, top):
        acc_buf[j, view] = acc
        top_buf[j, view] = jnp.broadcast_to(top, (tokens, cols))

    def merge(j, view, acc, top):
        old = top_buf[j, view][:, :1]
        new = jnp.maximum(old, top)
        return acc_buf[j, view] * jnp.exp(old - new) + acc * jnp.exp(top - new), new

    def put(n, slab):
        cat[n * tokens : (n + 1) * tokens, :cols] = slab

    def relay_step(step, carry):
        @pl.when(step < views)
        def _():
            view = visit(step)

            @pl.when(step >= 1)
            def _():
                kv_from(view, 0).wait_recv()

            kv_from(view, 1).wait_recv()
            halo(view).start()

        @pl.when((step >= 1) & (step <= views))
        def _():
            view = visit(step + views - 1)
            halo(view).wait_recv()
            cross(view).start()

        @pl.when(step >= LAG)
        def _():
            view = visit(step + views - LAG)

            @pl.when(step > LAG)
            def _():
                q_from(view, 0).wait_recv()

            q_from(view, 1).wait_recv()
            rows = []
            for j in range(2):
                put(j, kv_near[j, view])
                rows.append(bias_row(j * views + view, 1))
            for j in range(2):
                store(j, view, *attend(query(j, view), rows, 2))

        return carry

    lax.fori_loop(0, views + LAG, relay_step, 0)

    hard, easy = upper, 1 - upper

    def near_step(i, carry):
        view = (me + 1 + i) % views
        for j, count, own in ((hard, HARD, False), (easy, EASY, True)):
            rows = []
            if own:
                put(0, kv_near[2 + upper, view])
                rows.append(bias_row((2 + upper) * views + view, 1))
            for n in range(count):
                code = table[2 * view + j, n]
                index, valid = code % VALID, code // VALID
                put(len(rows), kv_near[index // views, index % views])
                rows.append(bias_row(index, valid))
            acc, top = attend(query(j, view), rows, len(rows))
            store(j, view, *merge(j, view, acc, top))
        return carry

    lax.fori_loop(0, views, near_step, 0)

    for step in range(views):
        cross(visit(step)).wait_recv()

    def far_step(i, carry):
        view = (me + 1 + i) % views
        for j, count, own in ((hard, HARD, True), (easy, EASY, False)):
            rows = []
            if own:
                there = jnp.where(upper > 0, jnp.where(base + 2 < bands, 1, 0), jnp.where(base > 0, 1, 0))
                put(0, kv_far[1 - upper, view])
                rows.append(bias_row((5 - upper) * views + view, there))
            for n in range(count, LISTED):
                code = table[2 * view + j, n]
                index, valid = code % VALID, code // VALID
                near_index = jnp.minimum(index, 4 * views - 1)
                far_index = jnp.maximum(index - 4 * views, 0)
                near = kv_near[near_index // views, near_index % views]
                far = kv_far[far_index // views, far_index % views]
                put(len(rows), jnp.where(index < 4 * views, near, far))
                rows.append(bias_row(index, valid))
            acc, top = attend(query(j, view), rows, len(rows))
            total, _ = merge(j, view, acc, top)
            blend = total[:, :cols] / total[:, cols:]
            o_send[j, view] = jnp.where(low_part, turn(blend[:part_rows]), blend[part_rows:]).astype(jnp.bfloat16)

            @pl.when((i < views - 1) | (j != odd))
            def _():
                o_to(view, j).start()

        return carry

    lax.fori_loop(0, views, far_step, 0)
    o_buf[2 * me + head] = o_send[odd, me]
    wo_load.wait()
    for view in others:
        o_from(view, 0).wait_recv()
    for view in [me, *others]:
        o_from(view, 1).wait_recv()

    total = row.astype(jnp.float32)
    for c in range(chips):
        groups = []
        for g in (2 * c, 2 * c + 1):
            a, b = o_buf[2 * g].astype(jnp.float32), o_buf[2 * g + 1].astype(jnp.float32)
            groups.append(
                jnp.concatenate([jnp.where(low_part, a, turn(b)), jnp.where(low_part, turn(a), b)], axis=0)
            )
        both = jnp.concatenate(groups, axis=1).astype(jnp.bfloat16)
        total = total + jnp.dot(both, wo_buf[c * wide : (c + 1) * wide], preferred_element_type=jnp.float32)
    out[...] = total

    for view in others:
        for theirs in range(2):
            kv_to(view, theirs).wait_send()
            q_to(view, theirs).wait_send()
        for j in range(2):
            o_to(view, j).wait_send()
    kv_to(me, 1).wait_send()
    q_to(me, 1).wait_send()
    o_to(me, 1 - odd).wait_send()
    for view in [me, *others]:
        halo(view).wait_send()
        cross(view).wait_send()


def epipolar_table(epipolar_bands, band, views):
    place = band % RING
    base, upper = band - place % 2, place // 2
    listed = lax.dynamic_slice_in_dim(epipolar_bands, base, 2, axis=1)
    numbers = jnp.arange(views, dtype=jnp.int32)
    own = (numbers[:, None] == numbers[None, :])[:, None, :]
    present = (listed >= 0) & ~own
    far = jnp.where(present, listed - base, 0)
    after, before = jnp.where(upper > 0, 2, 1), jnp.where(upper > 0, 1, 2)
    group = jnp.where(far > 1, after, jnp.where(far < 0, before, 0))
    code = (2 * group + (far + 2) % 2) * views + numbers + jnp.where(present, VALID, 0)
    key = jnp.where(own, 3, group) * views + numbers
    rank = jnp.sum((key[:, :, None, :] < key[:, :, :, None]).astype(jnp.int32), axis=3)
    chosen = rank[:, :, :, None] == numbers
    return jnp.sum(jnp.where(chosen, code[:, :, :, None], 0), axis=2).reshape(2 * views, views)


def body(latents, w_qkv, w_out, epipolar_bands, object_token_mask):
    views = lax.axis_size("view")
    bands = lax.axis_size("band")
    tokens, width = latents.shape[1:]
    cols = width // views
    table = epipolar_table(epipolar_bands, lax.axis_index("band"), views)
    bf16, f32 = jnp.bfloat16, jnp.float32
    dma = pltpu.SemaphoreType.DMA
    vmem = pl.BlockSpec(memory_space=pltpu.VMEM)
    hbm = pl.BlockSpec(memory_space=pltpu.HBM)
    updated = pl.pallas_call(
        functools.partial(kernel, views, bands),
        out_shape=jax.ShapeDtypeStruct((tokens, width), f32),
        in_specs=[pl.BlockSpec(memory_space=pltpu.SMEM), vmem, hbm, hbm, hbm],
        out_specs=vmem,
        scratch_shapes=[
            pltpu.VMEM((views // 2, 3, width, 2 * cols), bf16),
            pltpu.VMEM((width, width), bf16),
            pltpu.VMEM((6 * views, tokens), jnp.int32),
            pltpu.VMEM((views, 2, tokens, cols), bf16),
            pltpu.VMEM((views, 2, tokens // 2, cols), bf16),
            pltpu.VMEM((4, views, tokens, cols), bf16),
            pltpu.VMEM((2, views, tokens, cols), bf16),
            pltpu.VMEM((2, views, tokens // 2, cols), bf16),
            pltpu.VMEM(((1 + EASY) * tokens, 2 * cols), bf16),
            pltpu.VMEM((2, views, tokens, 2 * cols), f32),
            pltpu.VMEM((2, views, tokens, cols), f32),
            pltpu.VMEM((2, views, tokens // 2, cols), bf16),
            pltpu.VMEM((2 * views, tokens // 2, cols), bf16),
            dma((views // 2, 3)),
            dma,
            dma((6,)),
            dma((views, 2)),
            dma((2, views)),
            dma((views, 2)),
            dma((2, views)),
            dma((views,)),
            dma((views,)),
            dma((views,)),
            dma((views,)),
            dma((2, views)),
            dma((2 * views,)),
        ],
        compiler_params=pltpu.CompilerParams(
            collective_id=0, has_side_effects=True, vmem_limit_bytes=60 * 2**20
        ),
    )(table, latents[0], w_qkv, w_out, object_token_mask)
    return updated[None]


def solution(mesh):
    placed = (P("view", "band", None), P(), P(), P(), P())
    return jax.shard_map(
        body, mesh=mesh, in_specs=placed, out_specs=P("view", "band", None), check_vma=False
    )
```

time: 84 us -> 78.9 us (0.939)
  the two profiles are of different devices: /device:TPU:1 before, /device:TPU:15 now
where the time goes in v3:
time: 78.9 us; the launch traced here: 78.7 us
  Pallas kernels  74.2 us (94%)
  local copies, waits for them, and re-layouts  3.26 us (4%)
  other arithmetic  1.19 us (2%)
    pallas_call x1, Pallas kernels, body(): pl.pallas_call(functools.partial(kernel, views, bands), out_shape=jax.Sha...  74.2 us
    unnamed x4, local copies, waits for them, and re-layouts  3.18 us

profile of v3, /device:TPU:15, one launch (start us, length us, event | category | flops | bytes accessed | tf_op | source)
XLA Modules:
  0.0 78.7 jit_solution(12684123885400483652)
XLA Ops:
  0.0 0.0 copy-start
  0.0 0.7 copy-done
  0.8 0.1 constant_dynamic-slice_fusion
  0.8 0.1 copy.16
  1.0 0.4 convert_reduce_fusion
  1.5 0.7 select_reduce_fusion
  2.2 74.2 %shard_map.55 = f32[256,1024]{1,0:T(8,128)} custom-call(s32[16,8]{1,0:T(8,128)} %bitcast.5, bf16[256,1024]{1,0:T(8,128)(2,1)} %bitcast.4, bf16[1024,3072]{1,0:T(8,128)(2,1)} %w_qkv.1, bf16[1024,1024]{1,0:T(8,128)(2,1)} %w_out.1, s32[8,8192]{1,0:T(8,128)} %mask.1), custom_call_target="tpu_custom_call" | custom-call | tf_op jit(solution)/shard_map/pallas_call | solution.py:374
  76.4 2.3 %copy.18 = f32[1,256,1024]{2,1,0:T(8,128)} copy(f32[1,256,1024]{2,1,0:T(8,128)} %bitcast.3) | data formatting | bytes 2097152
  (4 shorter events, 0.0 us)
Async XLA Ops:
  0.0 0.8 copy-start

commit v4 on v3

--- a/solution.py
+++ b/solution.py
@@ -14,18 +14,20 @@
 LISTED = 7
 HARD = 3
 EASY = 5
-LAG = 4
+FIRST = 1
+AT_ONCE = 1
+CATS = 2 * AT_ONCE
 BIG = -1e30
 VALID = 64
 
 
 def kernel(
     views, bands, table, lat, w_qkv, w_out, mask, out,
-    w_buf, wo_buf, mask_buf, kv_send, q_send, kv_near, kv_far, q_buf, cat,
-    acc_buf, top_buf, o_send, o_buf,
-    w_sem, wo_sem, mask_sem, kv_ssem, kv_rsem, q_ssem, q_rsem, halo_ssem, halo_rsem, cross_ssem, cross_rsem,
-    o_ssem, o_rsem,
+    w_buf, wo_buf, mask_buf, kv_send, q_send, kv_own, kv_side, kv_far, q_buf, *rest,
 ):
+    cats = rest[:CATS]
+    (acc_buf, top_buf, o_send, o_buf, w_sem, wo_sem, mask_sem, kv_ssem, kv_rsem, q_ssem, q_rsem, halo_ssem, halo_rsem,
+     cross_ssem, cross_rsem, o_ssem, o_rsem) = rest[CATS:]
     tokens, width = lat.shape
     part_rows = tokens // 2
     cols = width // views
@@ -95,7 +97,7 @@
     def kv_to(view, theirs):
         h = (head + theirs) % 2
         return copy(
-            kv_send.at[view, h], kv_near.at[odd, me], kv_ssem.at[view, h], kv_rsem.at[odd, me],
+            kv_send.at[view, h], kv_own.at[odd, me], kv_ssem.at[view, h], kv_rsem.at[odd, me],
             view, partner if theirs else band,
         )
 
@@ -108,7 +110,7 @@
 
     def kv_from(view, theirs):
         j = (odd + theirs) % 2
-        at = kv_near.at[j, view]
+        at = kv_own.at[j, view]
         return copy(at, at, kv_ssem.at[view, 0], kv_rsem.at[j, view], me, partner)
 
     def q_from(view, theirs):
@@ -118,13 +120,13 @@
 
     def halo(view):
         return copy(
-            kv_near.at[pl.ds(0, 2), view], kv_near.at[pl.ds(2, 2), view], halo_ssem.at[view], halo_rsem.at[view],
+            kv_own.at[pl.ds(0, 2), view], kv_side.at[pl.ds(0, 2), view], halo_ssem.at[view], halo_rsem.at[view],
             me, across,
         )
 
     def cross(view):
         return copy(
-            kv_near.at[pl.ds(2, 2), view], kv_far.at[pl.ds(0, 2), view], cross_ssem.at[view], cross_rsem.at[view],
+            kv_side.at[pl.ds(0, 2), view], kv_far.at[pl.ds(0, 2), view], cross_ssem.at[view], cross_rsem.at[view],
             me, beyond,
         )
 
@@ -161,7 +163,7 @@
             kv_send[2 * there + c, 0] = jnp.where(low, k, turn(v)).astype(jnp.bfloat16)
             kv_send[2 * there + c, 1] = jnp.where(low, turn(k), v).astype(jnp.bfloat16)
         if n == 0:
-            kv_near[odd, me] = kv_send[me, head]
+            kv_own[odd, me] = kv_send[me, head]
             pl.semaphore_wait(barrier, 2 * views + 2)
             kv_to(me, 1).start()
             for theirs in range(2):
@@ -188,7 +190,8 @@
 
     for load in masks:
         load.wait()
-    cat[:, cols:] = jnp.ones((cat.shape[0], cols), jnp.bfloat16)
+    for cat in cats:
+        cat[:, cols:] = jnp.ones((cat.shape[0], cols), jnp.bfloat16)
 
     def bias_row(index, valid):
         seen = mask_buf[pl.ds(index, 1), :] * valid
@@ -199,7 +202,7 @@
         rows = jnp.concatenate([jnp.where(low_part, both, 0.0), jnp.where(low_part, turn(both), 0.0)], axis=0)
         return rows.astype(jnp.bfloat16)
 
-    def attend(q, rows, count):
+    def attend(cat, q, rows, count):
         keys = count * tokens
         s = lax.dot_general(
             q, cat[:keys, :cols], (((1,), (1,)), ((), ())), preferred_element_type=jnp.float32
@@ -218,99 +221,99 @@
         new = jnp.maximum(old, top)
         return acc_buf[j, view] * jnp.exp(old - new) + acc * jnp.exp(top - new), new
 
-    def put(n, slab):
-        cat[n * tokens : (n + 1) * tokens, :cols] = slab
+    hard, easy = upper, 1 - upper
+
+    def gather(cat, spots, listed, held):
+        rows = []
+        for slab, index, valid in spots:
+            cat[len(rows) * tokens : (len(rows) + 1) * tokens, :cols] = slab
+            rows.append(bias_row(index, valid))
+        for code in listed:
+            index, valid = code % VALID, code // VALID
+            pick, view = index // views, index % views
+            slab = held[0][pick % 2, view]
+            for group in range(1, len(held)):
+                slab = jnp.where(pick // 2 == group, held[group][pick % 2, view], slab)
+            cat[len(rows) * tokens : (len(rows) + 1) * tokens, :cols] = slab
+            rows.append(bias_row(index, valid))
+        return rows
 
     def relay_step(step, carry):
-        @pl.when(step < views)
+        view = visit(step)
+
+        @pl.when(step >= 1)
         def _():
-            view = visit(step)
-
-            @pl.when(step >= 1)
-            def _():
-                kv_from(view, 0).wait_recv()
-
-            kv_from(view, 1).wait_recv()
-            halo(view).start()
-
-        @pl.when((step >= 1) & (step <= views))
+            kv_from(view, 0).wait_recv()
+
+        kv_from(view, 1).wait_recv()
+        halo(view).start()
+        return carry
+
+    lax.fori_loop(0, views, relay_step, 0)
+
+    def own_step(step, carry):
+        view = visit(step)
+        halo(view).wait_recv()
+        cross(view).start()
+
+        @pl.when(step >= 1)
         def _():
-            view = visit(step + views - 1)
-            halo(view).wait_recv()
-            cross(view).start()
-
-        @pl.when(step >= LAG)
-        def _():
-            view = visit(step + views - LAG)
-
-            @pl.when(step > LAG)
-            def _():
-                q_from(view, 0).wait_recv()
-
-            q_from(view, 1).wait_recv()
-            rows = []
-            for j in range(2):
-                put(j, kv_near[j, view])
-                rows.append(bias_row(j * views + view, 1))
-            for j in range(2):
-                store(j, view, *attend(query(j, view), rows, 2))
-
+            q_from(view, 0).wait_recv()
+
+        q_from(view, 1).wait_recv()
+        for n, j in enumerate((hard, easy)):
+            spots = [(kv_own[0, view], view, 1), (kv_own[1, view], views + view, 1)]
+            if n == 1:
+                spots.append((kv_side[upper, view], (2 + upper) * views + view, 1))
+            rows = gather(cats[n], spots, [table[2 * view + j, r] for r in range(FIRST)], (kv_own,))
+            store(j, view, *attend(cats[n], query(j, view), rows, len(rows)))
         return carry
 
-    lax.fori_loop(0, views + LAG, relay_step, 0)
-
-    hard, easy = upper, 1 - upper
+    lax.fori_loop(0, views, own_step, 0)
 
     def near_step(i, carry):
-        view = (me + 1 + i) % views
-        for j, count, own in ((hard, HARD, False), (easy, EASY, True)):
-            rows = []
-            if own:
-                put(0, kv_near[2 + upper, view])
-                rows.append(bias_row((2 + upper) * views + view, 1))
-            for n in range(count):
-                code = table[2 * view + j, n]
-                index, valid = code % VALID, code // VALID
-                put(len(rows), kv_near[index // views, index % views])
-                rows.append(bias_row(index, valid))
-            acc, top = attend(query(j, view), rows, len(rows))
-            store(j, view, *merge(j, view, acc, top))
+        for turn_ in range(AT_ONCE):
+            view = (me + 1 + AT_ONCE * i + turn_) % views
+            for n, (j, count) in enumerate(((hard, HARD), (easy, EASY))):
+                cat = cats[2 * turn_ + n]
+                rows = gather(cat, [], [table[2 * view + j, r] for r in range(FIRST, count)], (kv_own, kv_side))
+                acc, top = attend(cat, query(j, view), rows, len(rows))
+                store(j, view, *merge(j, view, acc, top))
         return carry
 
-    lax.fori_loop(0, views, near_step, 0)
+    lax.fori_loop(0, views // AT_ONCE, near_step, 0)
 
     for step in range(views):
         cross(visit(step)).wait_recv()
 
     def far_step(i, carry):
-        view = (me + 1 + i) % views
-        for j, count, own in ((hard, HARD, True), (easy, EASY, False)):
-            rows = []
-            if own:
-                there = jnp.where(upper > 0, jnp.where(base + 2 < bands, 1, 0), jnp.where(base > 0, 1, 0))
-                put(0, kv_far[1 - upper, view])
-                rows.append(bias_row((5 - upper) * views + view, there))
-            for n in range(count, LISTED):
-                code = table[2 * view + j, n]
-                index, valid = code % VALID, code // VALID
-                near_index = jnp.minimum(index, 4 * views - 1)
-                far_index = jnp.maximum(index - 4 * views, 0)
-                near = kv_near[near_index // views, near_index % views]
-                far = kv_far[far_index // views, far_index % views]
-                put(len(rows), jnp.where(index < 4 * views, near, far))
-                rows.append(bias_row(index, valid))
-            acc, top = attend(query(j, view), rows, len(rows))
-            total, _ = merge(j, view, acc, top)
-            blend = total[:, :cols] / total[:, cols:]
-            o_send[j, view] = jnp.where(low_part, turn(blend[:part_rows]), blend[part_rows:]).astype(jnp.bfloat16)
-
-            @pl.when((i < views - 1) | (j != odd))
+        for turn_ in range(AT_ONCE):
+            view = (me + 1 + AT_ONCE * i + turn_) % views
+            for n, (j, count) in enumerate(((hard, HARD), (easy, EASY))):
+                cat = cats[2 * turn_ + n]
+                spots = []
+                if n == 0:
+                    there = jnp.where(upper > 0, jnp.where(base + 2 < bands, 1, 0), jnp.where(base > 0, 1, 0))
+                    spots.append((kv_far[1 - upper, view], (5 - upper) * views + view, there))
+                listed = [table[2 * view + j, r] for r in range(count, LISTED)]
+                rows = gather(cat, spots, listed, (kv_own, kv_side, kv_far))
+                acc, top = attend(cat, query(j, view), rows, len(rows))
+                total, _ = merge(j, view, acc, top)
+                blend = total[:, :cols] / total[:, cols:]
+                packed = jnp.where(low_part, turn(blend[:part_rows]), blend[part_rows:])
+                o_send[j, view] = packed.astype(jnp.bfloat16)
+        for turn_ in range(AT_ONCE):
+            nth = AT_ONCE * i + turn_
+            view = (me + 1 + nth) % views
+            o_to(view, 1 - odd).start()
+
+            @pl.when(nth < views - 1)
             def _():
-                o_to(view, j).start()
+                o_to(view, odd).start()
 
         return carry
 
-    lax.fori_loop(0, views, far_step, 0)
+    lax.fori_loop(0, views // AT_ONCE, far_step, 0)
     o_buf[2 * me + head] = o_send[odd, me]
     wo_load.wait()
     for view in others:
@@ -382,10 +385,9 @@
             pltpu.VMEM((6 * views, tokens), jnp.int32),
             pltpu.VMEM((views, 2, tokens, cols), bf16),
             pltpu.VMEM((views, 2, tokens // 2, cols), bf16),
-            pltpu.VMEM((4, views, tokens, cols), bf16),
-            pltpu.VMEM((2, views, tokens, cols), bf16),
+            *[pltpu.VMEM((2, views, tokens, cols), bf16) for _ in range(3)],
             pltpu.VMEM((2, views, tokens // 2, cols), bf16),
-            pltpu.VMEM(((1 + EASY) * tokens, 2 * cols), bf16),
+            *[pltpu.VMEM(((LISTED - 1) * tokens, 2 * cols), bf16) for _ in range(CATS)],
             pltpu.VMEM((2, views, tokens, 2 * cols), f32),
             pltpu.VMEM((2, views, tokens, cols), f32),
             pltpu.VMEM((2, views, tokens // 2, cols), bf16),

time: 78.9 us -> 69.1 us (0.88)
  the two profiles are of different devices: /device:TPU:15 before, /device:TPU:1 now
where the time goes in v4:
time: 69.1 us; the launch traced here: 68.9 us
  Pallas kernels  64.4 us (93%)
  local copies, waits for them, and re-layouts  3.26 us (5%)
  other arithmetic  1.19 us (2%)
    pallas_call x1, Pallas kernels, body(): pl.pallas_call(functools.partial(kernel, views, bands), out_shape=jax.Sha...  64.4 us
    unnamed x4, local copies, waits for them, and re-layouts  3.18 us

profile of v4, /device:TPU:1, one launch (start us, length us, event | category | flops | bytes accessed | tf_op | source)
XLA Modules:
  0.0 68.9 jit_solution(7525724930827348375)
XLA Ops:
  0.0 0.0 copy-start
  0.0 0.7 %copy-done = s32[8,32,8]{1,2,0:T(8,128)S(1)} copy-done((s32[8,32,8]{1,2,0:T(8,128)S(1)}, s32[8,32,8]{1,2,0:T(8,128)}, u32[]{:S(2)}) %copy-start) | copy-done | bytes 8216
  0.8 0.1 constant_dynamic-slice_fusion
  0.8 0.1 copy.16
  1.0 0.4 convert_reduce_fusion
  1.5 0.7 %select_reduce_fusion = s32[8,2,8]{2,1,0:T(2,128)} fusion(s32[8,2,8]{2,1,0:T(2,128)S(1)} %copy.15, s32[8,2,8]{2,1,0:T(2,128)S(1)} %convert_reduce_fusion), kind=kLoop, calls=%fused_computation | loop fusion | flops 2944 | bytes 1536 | tf_op jit(solution)/shard_map/reduce_sum | solution.py:364
  2.2 64.4 %shard_map.55 = f32[256,1024]{1,0:T(8,128)} custom-call(s32[16,8]{1,0:T(8,128)} %bitcast.5, bf16[256,1024]{1,0:T(8,128)(2,1)} %bitcast.4, bf16[1024,3072]{1,0:T(8,128)(2,1)} %w_qkv.1, bf16[1024,1024]{1,0:T(8,128)(2,1)} %w_out.1, s32[8,8192]{1,0:T(8,128)} %mask.1), custom_call_target="tpu_custom_call" | custom-call | tf_op jit(solution)/shard_map/pallas_call | solution.py:377
  66.6 2.3 %copy.18 = f32[1,256,1024]{2,1,0:T(8,128)} copy(f32[1,256,1024]{2,1,0:T(8,128)} %bitcast.3) | data formatting | bytes 2097152
  (4 shorter events, 0.0 us)
Async XLA Ops:
  0.0 0.8 %copy-start = (s32[8,32,8]{1,2,0:T(8,128)S(1)}, s32[8,32,8]{1,2,0:T(8,128)}, u32[]{:S(2)}) copy-start(s32[8,32,8]{1,2,0:T(8,128)} %param.8) | copy-start | bytes 24580

commit v5 on v4

--- a/solution.py
+++ b/solution.py
@@ -22,13 +22,15 @@
 
 
 def kernel(
-    views, bands, table, lat, w_qkv, w_out, mask, out,
-    w_buf, wo_buf, mask_buf, kv_send, q_send, kv_own, kv_side, kv_far, q_buf, *rest,
+    views, bands, listing, lat_hbm, w_qkv, mask, out,
+    table, lat, w_buf, mask_buf, kv_send, q_send, kv_own, kv_side, kv_far, q_buf, *rest,
 ):
     cats = rest[:CATS]
-    (acc_buf, top_buf, o_send, o_buf, w_sem, wo_sem, mask_sem, kv_ssem, kv_rsem, q_ssem, q_rsem, halo_ssem, halo_rsem,
+    (acc_buf, top_buf, o_send, o_buf, lat_sem, w_sem, mask_sem, kv_ssem, kv_rsem, q_ssem, q_rsem, halo_ssem, halo_rsem,
      cross_ssem, cross_rsem, o_ssem, o_rsem) = rest[CATS:]
     tokens, width = lat.shape
+    lat_load = pltpu.make_async_copy(lat_hbm, lat, lat_sem)
+    lat_load.start()
     part_rows = tokens // 2
     cols = width // views
     wide = 2 * cols
@@ -85,8 +87,6 @@
             )
             load.start()
             masks.append(load)
-    wo_load = pltpu.make_async_copy(w_out, wo_buf, wo_sem)
-    wo_load.start()
 
     def copy(src, dst, ssem, rsem, view, at):
         return pltpu.make_async_remote_copy(
@@ -140,6 +140,7 @@
         at = o_buf.at[slot]
         return copy(at, at, o_ssem.at[0, view], o_rsem.at[slot], me, partner)
 
+    lat_load.wait()
     row = lat[...]
     scale = HEAD_DIM**-0.5
     low = lax.broadcasted_iota(jnp.int32, (tokens, cols), 1) < HEAD_DIM
@@ -238,6 +239,25 @@
             rows.append(bias_row(index, valid))
         return rows
 
+    def order_list(n):
+        query_view, j = n // 2, n % 2
+        codes, keys = [], []
+        for off in range(1, views):
+            view = (query_view + off) % views
+            listed = listing[query_view, view, base + j]
+            present = jnp.where(listed >= 0, 1, 0)
+            far = present * (listed - base)
+            after, before = jnp.where(far > 1, 1, 0), jnp.where(far < 0, 1, 0)
+            group = (1 + upper) * after + (2 - upper) * before
+            second = jnp.where((far == 1) | (far == 3) | (far == -1), 1, 0)
+            codes.append((2 * group + second) * views + view + VALID * present)
+            keys.append(group * views + off)
+        ranks = []
+        for a in keys:
+            ranks.append(sum(jnp.where(b < a, 1, 0) for b in keys if b is not a))
+        for place_ in range(LISTED):
+            table[n, place_] = sum(jnp.where(r == place_, c, 0) for r, c in zip(ranks, codes))
+
     def relay_step(step, carry):
         view = visit(step)
 
@@ -247,6 +267,8 @@
 
         kv_from(view, 1).wait_recv()
         halo(view).start()
+        for j in range(2):
+            order_list(2 * step + j)
         return carry
 
     lax.fori_loop(0, views, relay_step, 0)
@@ -315,23 +337,15 @@
 
     lax.fori_loop(0, views // AT_ONCE, far_step, 0)
     o_buf[2 * me + head] = o_send[odd, me]
-    wo_load.wait()
     for view in others:
         o_from(view, 0).wait_recv()
     for view in [me, *others]:
         o_from(view, 1).wait_recv()
 
-    total = row.astype(jnp.float32)
-    for c in range(chips):
-        groups = []
-        for g in (2 * c, 2 * c + 1):
-            a, b = o_buf[2 * g].astype(jnp.float32), o_buf[2 * g + 1].astype(jnp.float32)
-            groups.append(
-                jnp.concatenate([jnp.where(low_part, a, turn(b)), jnp.where(low_part, turn(a), b)], axis=0)
-            )
-        both = jnp.concatenate(groups, axis=1).astype(jnp.bfloat16)
-        total = total + jnp.dot(both, wo_buf[c * wide : (c + 1) * wide], preferred_element_type=jnp.float32)
-    out[...] = total
+    for g in range(views):
+        a, b = o_buf[2 * g].astype(jnp.float32), o_buf[2 * g + 1].astype(jnp.float32)
+        both = jnp.concatenate([jnp.where(low_part, a, turn(b)), jnp.where(low_part, turn(a), b)], axis=0)
+        out[:, g * cols : (g + 1) * cols] = both.astype(jnp.bfloat16)
 
     for view in others:
         for theirs in range(2):
@@ -347,41 +361,24 @@
         cross(view).wait_send()
 
 
-def epipolar_table(epipolar_bands, band, views):
-    place = band % RING
-    base, upper = band - place % 2, place // 2
-    listed = lax.dynamic_slice_in_dim(epipolar_bands, base, 2, axis=1)
-    numbers = jnp.arange(views, dtype=jnp.int32)
-    own = (numbers[:, None] == numbers[None, :])[:, None, :]
-    present = (listed >= 0) & ~own
-    far = jnp.where(present, listed - base, 0)
-    after, before = jnp.where(upper > 0, 2, 1), jnp.where(upper > 0, 1, 2)
-    group = jnp.where(far > 1, after, jnp.where(far < 0, before, 0))
-    code = (2 * group + (far + 2) % 2) * views + numbers + jnp.where(present, VALID, 0)
-    key = jnp.where(own, 3, group) * views + numbers
-    rank = jnp.sum((key[:, :, None, :] < key[:, :, :, None]).astype(jnp.int32), axis=3)
-    chosen = rank[:, :, :, None] == numbers
-    return jnp.sum(jnp.where(chosen, code[:, :, :, None], 0), axis=2).reshape(2 * views, views)
-
-
 def body(latents, w_qkv, w_out, epipolar_bands, object_token_mask):
     views = lax.axis_size("view")
     bands = lax.axis_size("band")
     tokens, width = latents.shape[1:]
     cols = width // views
-    table = epipolar_table(epipolar_bands, lax.axis_index("band"), views)
     bf16, f32 = jnp.bfloat16, jnp.float32
     dma = pltpu.SemaphoreType.DMA
     vmem = pl.BlockSpec(memory_space=pltpu.VMEM)
     hbm = pl.BlockSpec(memory_space=pltpu.HBM)
-    updated = pl.pallas_call(
+    blended = pl.pallas_call(
         functools.partial(kernel, views, bands),
-        out_shape=jax.ShapeDtypeStruct((tokens, width), f32),
-        in_specs=[pl.BlockSpec(memory_space=pltpu.SMEM), vmem, hbm, hbm, hbm],
+        out_shape=jax.ShapeDtypeStruct((tokens, width), bf16),
+        in_specs=[pl.BlockSpec(memory_space=pltpu.SMEM), hbm, hbm, hbm],
         out_specs=vmem,
         scratch_shapes=[
+            pltpu.SMEM((2 * views, LISTED), jnp.int32),
+            pltpu.VMEM((tokens, width), bf16),
             pltpu.VMEM((views // 2, 3, width, 2 * cols), bf16),
-            pltpu.VMEM((width, width), bf16),
             pltpu.VMEM((6 * views, tokens), jnp.int32),
             pltpu.VMEM((views, 2, tokens, cols), bf16),
             pltpu.VMEM((views, 2, tokens // 2, cols), bf16),
@@ -392,8 +389,8 @@
             pltpu.VMEM((2, views, tokens, cols), f32),
             pltpu.VMEM((2, views, tokens // 2, cols), bf16),
             pltpu.VMEM((2 * views, tokens // 2, cols), bf16),
+            dma,
             dma((views // 2, 3)),
-            dma,
             dma((6,)),
             dma((views, 2)),
             dma((2, views)),
@@ -409,7 +406,8 @@
         compiler_params=pltpu.CompilerParams(
             collective_id=0, has_side_effects=True, vmem_limit_bytes=60 * 2**20
         ),
-    )(table, latents[0], w_qkv, w_out, object_token_mask)
+    )(epipolar_bands.transpose(0, 2, 1), latents[0], w_qkv, object_token_mask)
+    updated = latents[0].astype(f32) + jnp.dot(blended, w_out, preferred_element_type=f32)
     return updated[None]
 
 

time: 69.1 us -> 67.6 us (0.978)
  local copies, waits for them, and re-layouts: 3.26 us -> 0.01 us
  matrix products: 0 us -> 2.72 us
  other arithmetic: 1.19 us -> 0 us
    unnamed x4, local copies, waits for them, and re-layouts: 3.18 us -> 0.01 us
    dot_general x0 -> x1, matrix products: none -> 2.72 us  [body(): jnp.dot(blended, w_out, preferred_element_type=f32)]
    reduce_sum x2 -> x0, other arithmetic: 1.15 us -> none  [the longest x1 0.72 us: epipolar_table(): jnp.sum(jnp.where(chosen, code[:, :, :, None], 0), axis=2)]
where the time goes in v5:
time: 67.6 us; the launch traced here: 67.4 us
  Pallas kernels  64.7 us (96%)
  matrix products  2.72 us (4%)
    pallas_call x1, Pallas kernels, body(): pl.pallas_call(functools.partial(kernel, views, bands), out_shape=jax.Sha...  64.7 us
    dot_general x1, matrix products, body(): jnp.dot(blended, w_out, preferred_element_type=f32)  2.72 us

profile of v5, /device:TPU:1, one launch (start us, length us, event | category | flops | bytes accessed | tf_op | source)
XLA Modules:
  0.0 67.4 jit_solution(8047809579994524441)
XLA Ops:
  0.0 0.0 copy-start
  0.0 0.0 copy-start.1
  0.0 64.7 %shard_map.55 = bf16[256,1024]{1,0:T(8,128)(2,1)} custom-call(s32[8,8,32]{2,1,0:T(8,128)} %bitcast.8, bf16[256,1024]{1,0:T(8,128)(2,1)} %bitcast.7, bf16[1024,3072]{1,0:T(8,128)(2,1)} %w_qkv.1, s32[8,8192]{1,0:T(8,128)} %mask.1), custom_call_target="tpu_custom_call" | custom-call | tf_op jit(solution)/shard_map/pallas_call | solution.py:373
  64.7 0.0 copy-done
  64.7 0.0 copy-done.1
  64.7 2.7 %fusion = f32[1,256,1024]{2,1,0:T(8,128)} fusion(bf16[256,1024]{1,0:T(8,128)(2,1)} %shard_map.55, bf16[1024,1024]{1,0:T(8,128)(2,1)S(1)} %copy-done, bf16[1,256,1024]{2,1,0:T(8,128)(2,1)S(1)} %copy-done.1), kind=kOutput, calls=%fused_computation.1 | convolution fusion | flops 537395200 | bytes 4194304 | tf_op jit(solution)/shard_map/dot_general | solution.py:410
Async XLA Ops:
  0.0 64.7 %copy-start = (bf16[1024,1024]{1,0:T(8,128)(2,1)S(1)}, bf16[1024,1024]{1,0:T(8,128)(2,1)}, u32[]{:S(2)}) copy-start(bf16[1024,1024]{1,0:T(8,128)(2,1)} %param.7) | copy-start | bytes 6291460
  0.0 64.7 %copy-start.1 = (bf16[1,256,1024]{2,1,0:T(8,128)(2,1)S(1)}, bf16[1,256,1024]{2,1,0:T(8,128)(2,1)}, u32[]{:S(2)}) copy-start(bf16[1,256,1024]{2,1,0:T(8,128)(2,1)} %param.5) | copy-start | bytes 1572868

commit v6 on v5

--- a/solution.py
+++ b/solution.py
@@ -295,7 +295,7 @@
 
     def near_step(i, carry):
         for turn_ in range(AT_ONCE):
-            view = (me + 1 + AT_ONCE * i + turn_) % views
+            view = visit(views - 1 - AT_ONCE * i - turn_)
             for n, (j, count) in enumerate(((hard, HARD), (easy, EASY))):
                 cat = cats[2 * turn_ + n]
                 rows = gather(cat, [], [table[2 * view + j, r] for r in range(FIRST, count)], (kv_own, kv_side))
@@ -310,7 +310,7 @@
 
     def far_step(i, carry):
         for turn_ in range(AT_ONCE):
-            view = (me + 1 + AT_ONCE * i + turn_) % views
+            view = visit(views - 1 - AT_ONCE * i - turn_)
             for n, (j, count) in enumerate(((hard, HARD), (easy, EASY))):
                 cat = cats[2 * turn_ + n]
                 spots = []
@@ -326,7 +326,7 @@
                 o_send[j, view] = packed.astype(jnp.bfloat16)
         for turn_ in range(AT_ONCE):
             nth = AT_ONCE * i + turn_
-            view = (me + 1 + nth) % views
+            view = visit(views - 1 - nth)
             o_to(view, 1 - odd).start()
 
             @pl.when(nth < views - 1)

time: 67.6 us -> 67.6 us (level)
  no operation moved by 1% of the time
where the time goes in v6:
time: 67.6 us; the launch traced here: 67.4 us
  Pallas kernels  64.7 us (96%)
  matrix products  2.72 us (4%)
    pallas_call x1, Pallas kernels, body(): pl.pallas_call(functools.partial(kernel, views, bands), out_shape=jax.Sha...  64.7 us
    dot_general x1, matrix products, body(): jnp.dot(blended, w_out, preferred_element_type=f32)  2.72 us

profile of v6, /device:TPU:1, one launch (start us, length us, event | category | flops | bytes accessed | tf_op | source)
XLA Modules:
  0.0 67.4 jit_solution(6243221050722951939)
XLA Ops:
  0.0 0.0 copy-start
  0.0 0.0 copy-start.1
  0.0 64.7 %shard_map.55 = bf16[256,1024]{1,0:T(8,128)(2,1)} custom-call(s32[8,8,32]{2,1,0:T(8,128)} %bitcast.8, bf16[256,1024]{1,0:T(8,128)(2,1)} %bitcast.7, bf16[1024,3072]{1,0:T(8,128)(2,1)} %w_qkv.1, s32[8,8192]{1,0:T(8,128)} %mask.1), custom_call_target="tpu_custom_call" | custom-call | tf_op jit(solution)/shard_map/pallas_call | solution.py:373
  64.7 0.0 copy-done
  64.7 0.0 copy-done.1
  64.7 2.7 %fusion = f32[1,256,1024]{2,1,0:T(8,128)} fusion(bf16[256,1024]{1,0:T(8,128)(2,1)} %shard_map.55, bf16[1024,1024]{1,0:T(8,128)(2,1)S(1)} %copy-done, bf16[1,256,1024]{2,1,0:T(8,128)(2,1)S(1)} %copy-done.1), kind=kOutput, calls=%fused_computation.1 | convolution fusion | flops 537395200 | bytes 4194304 | tf_op jit(solution)/shard_map/dot_general | solution.py:410
Async XLA Ops:
  0.0 64.7 %copy-start = (bf16[1024,1024]{1,0:T(8,128)(2,1)S(1)}, bf16[1024,1024]{1,0:T(8,128)(2,1)}, u32[]{:S(2)}) copy-start(bf16[1024,1024]{1,0:T(8,128)(2,1)} %param.7) | copy-start | bytes 6291460
  0.0 64.7 %copy-start.1 = (bf16[1,256,1024]{2,1,0:T(8,128)(2,1)S(1)}, bf16[1,256,1024]{2,1,0:T(8,128)(2,1)}, u32[]{:S(2)}) copy-start(bf16[1,256,1024]{2,1,0:T(8,128)(2,1)} %param.5) | copy-start | bytes 1572868
